TPU v7x, 32 devices: a whole 2x2x4 slice. The times are simulated.
32 devices in a mesh: fsdp: 2 (over core), expert: 16 (over z, y, x).
Axes of the slice: x: 2, y: 2, z: 4, core: 2. Of those that a mesh axis runs over, the one named last changes fastest.
Arguments:
- tokens: bfloat16 [16, 256, 2048], P('expert', 'fsdp'), may hold values from -6 to 6
- norm1_gain: bfloat16 [2048], P(('fsdp', 'expert')), may hold values from 0.5 to 1.5
- q_weight: bfloat16 [2048, 3072], P(('fsdp', 'expert')), may hold values from -0.125 to 0.125
- kv_down: bfloat16 [2048, 576], P(('fsdp', 'expert')), may hold values from -0.125 to 0.125
- latent_gain: bfloat16 [512], P(('fsdp', 'expert')), may hold values from 0.5 to 1.5
- kv_up: bfloat16 [512, 4096], P(('fsdp', 'expert')), may hold values from -0.25 to 0.25
- o_weight: bfloat16 [2048, 2048], P(('fsdp', 'expert')), may hold values from -1 to 1
- norm2_gain: bfloat16 [2048], P(('fsdp', 'expert')), may hold values from 0.5 to 1.5
- router: bfloat16 [2048, 16], P(('fsdp', 'expert')), may hold values from -0.0625 to 0.0625
- shared_gate_up: bfloat16 [2048, 5632], P(('fsdp', 'expert')), may hold values from -0.125 to 0.125
- shared_down: bfloat16 [2816, 2048], P(('fsdp', 'expert')), may hold values from -0.109375 to 0.109375
- expert_gate_up: bfloat16 [16, 2048, 2816], P('expert', 'fsdp'), may hold values from -0.125 to 0.125
- expert_down: bfloat16 [16, 1408, 2048], P('expert', None, 'fsdp'), may hold values from -0.4375 to 0.4375
- teacher: bfloat16 [16, 256, 2048], P('expert', 'fsdp'), may hold values from -10 to 10
- routes: int32 [16, 256, 6], P('expert', 'fsdp'), may hold values from 0 to 15, all different within a row; in each aligned block of 128 rows (0 to 127, 128 to 255, ..., all dimensions but the last counted through in order) at most 80 rows name the same one
- prefix: int32 [16], P('expert'), may hold values from 25 to 128
- token_count: int32 [1], replicated, may hold values from 2048 to 4096
Outputs:
- mixed: bfloat16 [16, 256, 2048], P('expert', 'fsdp')
- loss_value: float32 [1], replicated
- grad_tokens: float32 [16, 256, 2048], P('expert', 'fsdp')
- grad_norm1_gain: float32 [2048], P(('fsdp', 'expert'))
- grad_q_weight: float32 [2048, 3072], P(('fsdp', 'expert'))
- grad_kv_down: float32 [2048, 576], P(('fsdp', 'expert'))
- grad_latent_gain: float32 [512], P(('fsdp', 'expert'))
- grad_kv_up: float32 [512, 4096], P(('fsdp', 'expert'))
- grad_o_weight: float32 [2048, 2048], P(('fsdp', 'expert'))
- grad_norm2_gain: float32 [2048], P(('fsdp', 'expert'))
- grad_router: float32 [2048, 16], P(('fsdp', 'expert'))
- grad_shared_gate_up: float32 [2048, 5632], P(('fsdp', 'expert'))
- grad_shared_down: float32 [2816, 2048], P(('fsdp', 'expert'))
- grad_expert_gate_up: float32 [16, 2048, 2816], P('expert', 'fsdp')
- grad_expert_down: float32 [16, 1408, 2048], P('expert', None, 'fsdp')
Inputs may be any that keep to these rules, and one draw needn't show every extreme that they name: `routes`: each token names 6 different experts. Among the 128 tokens of one device no expert is named by more than 80 tokens, and in every draw some expert is named by exactly 80 tokens of some device.
All inputs are finite; a program needn't handle non-finite values.
Results may differ from a plain program's by a relative error of at most 0.015.
Values may be sent and summed in bfloat16 or wider, within the bound.
No kernel may reach another device: no remote copies, remote signals or barrier semaphores. Data moves between devices by JAX's collectives and lax.ppermute only.
A program may use at most 448 MiB of HBM per device.

v0:
```python
import math

import jax
import jax.numpy as jnp
import numpy as np
from jax import lax
from jax.experimental import pallas as pl
from jax.experimental.layout import Layout, with_layout_constraint
from jax.experimental.pallas import tpu as pltpu
from jax.sharding import Mesh
from jax.sharding import PartitionSpec as P

NH = 16
DN = 128
DR = 64
DV = 128
KVR = 512
FFE = 1408
FFS = 2816
TOP = 6
PLANE = 4

BF = jnp.bfloat16
F32 = jnp.float32

epsilon = 1e-06


def rms_norm(values, gain_row):
    return (
        values * lax.rsqrt(jnp.mean(values * values, axis=-1, keepdims=True) + epsilon) * gain_row
    )


def norm_back(values, gain_row, incoming):
    factor = lax.rsqrt(jnp.mean(values * values, axis=-1, keepdims=True) + epsilon)
    scaled = incoming * gain_row
    grad_values = factor * scaled - values * (factor * factor * factor) * jnp.mean(
        scaled * values, axis=-1, keepdims=True
    )
    grad_gain = jnp.sum(incoming * values * factor, axis=0)
    return (grad_values, grad_gain)


def tables(position, rot_width):
    half_width = rot_width // 2
    frequency = 10000.0 ** (-2.0 * jnp.arange(half_width, dtype=F32) / rot_width)
    angles = position.astype(F32)[:, None] * frequency[None, :]
    return (jnp.cos(angles), jnp.sin(angles))


def unrotate(values, cosine, sine_table):
    half_width = values.shape[-1] // 2
    first_half = values[..., :half_width]
    second = values[..., half_width:]
    return jnp.concatenate(
        [first_half * cosine + second * sine_table, second * cosine - first_half * sine_table],
        axis=-1,
    )


def dot_plain(left_side, right_side):
    return jnp.dot(left_side, right_side, preferred_element_type=F32)


def dot_last(left_side, right_side):
    return lax.dot_general(
        left_side, right_side, (((1,), (1,)), ((), ())), preferred_element_type=F32
    )


def dot_first(left_side, right_side):
    return lax.dot_general(
        left_side, right_side, (((0,), (0,)), ((), ())), preferred_element_type=F32
    )


def straight(values):
    return with_layout_constraint(values, Layout(tuple(range(values.ndim))))


def after(values, *others):
    return lax.optimization_barrier((values,) + others)[0]


def stage(*values):
    return lax.optimization_barrier(values)


def hop(values, axis, distance):
    size = lax.axis_size(axis)
    moves = [(i, i ^ distance) for i in range(size)]
    return straight(lax.ppermute(straight(values), axis, moves))


def gather_plane(values):
    return [values] + [hop(values, "r", j) for j in range(1, PLANE)]


def scatter_plane(parts):
    moved = [hop(parts[j].astype(BF), "r", j) for j in range(1, PLANE)]
    return parts[0].astype(F32) + sum(part.astype(F32) for part in moved)


def scatter_sides(own, given):
    total = straight((own.astype(F32) + given.astype(F32)).astype(BF))
    return scatter_plane([total[j] for j in range(PLANE)])


def column_order(axis):
    return jnp.arange(lax.axis_size(axis), dtype=jnp.int32) ^ lax.axis_index(axis)


def both_cores(values):
    other = hop(values, "fsdp", 1)
    first = lax.axis_index("fsdp") == 0
    return jnp.concatenate(
        [jnp.where(first, values, other), jnp.where(first, other, values)], axis=0
    )


def by_column(parts):
    return jnp.take(parts.astype(BF), column_order("z"), axis=0, mode="clip")


def sum_columns(parts):
    moved = [hop(parts[k], "z", k) for k in range(1, lax.axis_size("z"))]
    return parts[0].astype(F32) + sum(part.astype(F32) for part in moved)


def gather_columns(values):
    spread = jnp.broadcast_to(values[None], (lax.axis_size("z"),) + values.shape)
    return lax.all_to_all(spread, "z", split_axis=0, concat_axis=0, tiled=True)


def gather_columns_apart(values):
    column = [values] + [hop(values, "z", k) for k in range(1, lax.axis_size("z"))]
    return jnp.take(jnp.stack(column, axis=0), column_order("z"), axis=0, mode="clip")


def all_order():
    return (column_order("z")[:, None] * PLANE + column_order("r")[None, :]).reshape(-1)


def swap_plane(parts):
    shape = parts.shape[1:]
    parts = jnp.take(parts, all_order(), axis=0, mode="clip")
    parts = parts.reshape((lax.axis_size("z"), PLANE) + shape)
    plane = [parts[:, 0]] + [hop(parts[:, j], "r", j) for j in range(1, PLANE)]
    return jnp.stack(plane, axis=1)


def swap_column(plane):
    depth = lax.axis_size("z")
    column = [plane[0]] + [hop(plane[k], "z", k) for k in range(1, depth)]
    column = jnp.stack(column, axis=0).reshape((depth * PLANE,) + plane.shape[2:])
    return jnp.take(column, all_order(), axis=0, mode="clip")


ROOM = 56 * 1024 * 1024


def whole(array):
    return pl.BlockSpec(array.shape, lambda *_: (0,) * array.ndim)


def sums_of_products(lefts, rights, tall, wide=None, kind=F32):
    height, width = lefts[0].shape[1], rights[0].shape[1]
    depth = sum(left.shape[0] for left in lefts)
    wide = width if wide is None else wide

    def stack(refs, into):
        start = 0
        for ref in refs:
            into[start : start + ref.shape[0], :] = ref[...]
            start += ref.shape[0]

    def body(*refs):
        out_ref, left_ref, right_ref = refs[-3:]

        @pl.when(pl.program_id(1) == 0)
        def _():
            stack(refs[len(lefts) : len(lefts) + len(rights)], right_ref)

        stack(refs[: len(lefts)], left_ref)
        out_ref[...] = dot_first(left_ref[...], right_ref[...]).astype(kind)

    return pl.pallas_call(
        body,
        grid=(width // wide, height // tall),
        in_specs=[pl.BlockSpec((left.shape[0], tall), lambda j, i: (0, i)) for left in lefts]
        + [pl.BlockSpec((right.shape[0], wide), lambda j, i: (0, j)) for right in rights],
        out_specs=pl.BlockSpec((tall, wide), lambda j, i: (i, j)),
        out_shape=jax.ShapeDtypeStruct((height, width), kind),
        scratch_shapes=[pltpu.VMEM((depth, tall), BF), pltpu.VMEM((depth, wide), BF)],
        compiler_params=pltpu.CompilerParams(vmem_limit_bytes=ROOM),
        cost_estimate=pl.CostEstimate(
            flops=2 * depth * height * width,
            bytes_accessed=2 * depth * (height + width) + 4 * height * width,
            transcendentals=0,
        ),
    )(*lefts, *rights)


def swiglu_parts(gate, up, incoming):
    sigmoid = jax.nn.sigmoid(gate)
    return (
        (incoming * up * sigmoid * (1.0 + gate * (1.0 - sigmoid))).astype(BF),
        (incoming * gate * sigmoid).astype(BF),
    )


TILE = 256
STRIP = 512
PARTS = 4


def spans(size, width):
    return [slice(start, min(start + width, size)) for start in range(0, size, width)]


class Copies:
    def __init__(self, semaphores):
        self.semaphores = semaphores
        self.used = 0

    def start(self, source, target):
        copy = pltpu.make_async_copy(source, target, self.semaphores.at[self.used])
        self.used += 1
        copy.start()
        return [copy]

    def start_rows(self, source, target):
        rows = source.shape[0]
        step = rows // PARTS
        copies = []
        for part in range(PARTS):
            span = pl.ds(part * step, step)
            copies += self.start(source.at[span, :], target.at[span, :])
        return copies


def wait(copies):
    for copy in copies:
        copy.wait()


def expert_forward(pieces, chosen, masks, mine, shared_router, both, down, shared_down):
    planes, rows, width = pieces[0].shape
    blocks, capacity = chosen.shape[:2]
    slots, flat_rows = blocks * capacity, blocks * rows
    hidden, units, experts = down.shape[0], shared_down.shape[0], mine.shape[1]
    strips = spans(width, STRIP)
    shapes = [
        ((slots, width), BF), ((slots, 2 * hidden), BF), ((slots, hidden), BF), ((slots, width), BF),
        ((flat_rows, 2 * units), BF), ((flat_rows, units), BF),
    ] + [((planes, rows, width), F32 if j == 0 else BF) for j in range(PLANE)]
    gate_shape = jax.ShapeDtypeStruct((flat_rows, 128), F32)

    def body(
        chosen_ref, masks_ref, mine_ref, piece_0, piece_1, piece_2, piece_3, router_hbm, both_hbm,
        down_hbm, shared_down_hbm,
        gates_ref, in_hbm, gu_hbm, act_hbm, out_hbm, shared_gu_hbm, shared_act_hbm,
        total_0, total_1, total_2, total_3,
        rows_ref, router_ref, both_ref, down_ref, shared_down_ref,
        in_ref, gu_ref, act_ref, out_ref, shared_gu_ref, shared_act_ref,
        sum_0, sum_1, sum_2, sum_3, semaphores,
    ):
        copies = Copies(semaphores)
        totals, sums = (total_0, total_1, total_2, total_3), (sum_0, sum_1, sum_2, sum_3)
        coming = []
        for j, piece in enumerate((piece_0, piece_1, piece_2, piece_3)):
            for k in range(planes):
                target = rows_ref.at[pl.ds((j * planes + k) * rows, rows), :]
                coming.append(copies.start(piece.at[k], target))
        router_in = copies.start_rows(router_hbm, router_ref)
        both_in = copies.start_rows(both_hbm, both_ref)
        down_in = copies.start_rows(down_hbm, down_ref)
        down_in += copies.start(shared_down_hbm, shared_down_ref)
        for block in range(blocks):
            wait(coming[block])
            in_ref[block * capacity : (block + 1) * capacity, :] = dot_plain(
                chosen_ref[block], rows_ref[block * rows : (block + 1) * rows, :]
            ).astype(BF)
        leaving = copies.start(in_ref, in_hbm)
        wait(router_in)
        joined = dot_plain(rows_ref[...], router_ref[...])
        gate, up = joined[:, :units], joined[:, units : 2 * units]
        shared_gu_ref[...] = joined[:, : 2 * units].astype(BF)
        shared_act_ref[...] = (gate * jax.nn.sigmoid(gate) * up).astype(BF)
        leaving += copies.start(shared_gu_ref, shared_gu_hbm)
        leaving += copies.start(shared_act_ref, shared_act_hbm)
        mask = masks_ref[...] > 0.0
        logits = jnp.where(mask, joined[:, 2 * units : 2 * units + experts], -1e30)
        odds = jnp.exp(logits - jnp.max(logits, axis=1, keepdims=True))
        odds = jnp.where(mask, odds, 0.0)
        own = jnp.sum(odds * mine_ref[...], axis=1, keepdims=True)
        own = own / jnp.sum(odds, axis=1, keepdims=True)
        gates_ref[...] = jnp.broadcast_to(own, gates_ref.shape)
        wait(both_in)
        for span in spans(hidden, TILE):
            above = slice(hidden + span.start, hidden + span.stop)
            gate = dot_plain(in_ref[...], both_ref[:, span])
            up = dot_plain(in_ref[...], both_ref[:, above])
            gu_ref[:, span] = gate.astype(BF)
            gu_ref[:, above] = up.astype(BF)
            act_ref[:, span] = (gate * jax.nn.sigmoid(gate) * up).astype(BF)
        leaving += copies.start(gu_ref, gu_hbm)
        leaving += copies.start(act_ref, act_hbm)
        wait(down_in)
        for strip in strips:
            out_ref[:, strip] = dot_plain(act_ref[...], down_ref[:, strip]).astype(BF)
            shared = dot_plain(shared_act_ref[...], shared_down_ref[:, strip])
            for j in range(PLANE):
                for k in range(planes):
                    block = j * planes + k
                    span = slice(block * rows, (block + 1) * rows)
                    picked = dot_first(
                        chosen_ref[block], out_ref[block * capacity : (block + 1) * capacity, strip]
                    )
                    sums[j][k, :, strip] = (gates_ref[span, 0:1] * picked + shared[span, :]).astype(
                        sums[j].dtype
                    )
                place = pl.ds(strip.start, strip.stop - strip.start)
                leaving += copies.start(sums[j].at[:, :, place], totals[j].at[:, :, place])
        leaving += copies.start(out_ref, out_hbm)
        wait(leaving)

    anywhere = pl.BlockSpec(memory_space=pl.ANY)
    moved = [shared_router, both, down, shared_down]
    scratch = [pltpu.VMEM((flat_rows, width), BF)]
    scratch += [pltpu.VMEM(array.shape, BF) for array in moved]
    scratch += [pltpu.VMEM(*shape) for shape in shapes]
    count = blocks + 3 * PARTS + 1 + 6 + PLANE * len(strips)
    return pl.pallas_call(
        body,
        in_specs=[pl.BlockSpec(memory_space=pltpu.VMEM)] * 3 + [anywhere] * (PLANE + len(moved)),
        out_specs=[pl.BlockSpec(memory_space=pltpu.VMEM)] + [anywhere] * len(shapes),
        out_shape=[gate_shape] + [jax.ShapeDtypeStruct(*shape) for shape in shapes],
        scratch_shapes=scratch + [pltpu.SemaphoreType.DMA((count,))],
        compiler_params=pltpu.CompilerParams(vmem_limit_bytes=ROOM),
        cost_estimate=pl.CostEstimate(
            flops=2 * width * (3 * slots * hidden + flat_rows * 4 * units),
            bytes_accessed=2 * width * (3 * hidden + 4 * units + 4 * flat_rows) + 12 * slots * hidden,
            transcendentals=slots * hidden,
        ),
    )(chosen, masks, mine, *pieces, *moved)


def expert_backward(pieces, chosen, gates, gu, out, shared_gu, shared_router, both, down, shared_down):
    planes, rows, width = pieces[0].shape
    blocks, capacity = chosen.shape[:2]
    slots, flat_rows = blocks * capacity, blocks * rows
    hidden, units = down.shape[0], shared_down.shape[0]
    strips = spans(width, STRIP)
    shapes = [
        ((slots, width), BF), ((slots, 2 * hidden), BF), ((flat_rows, 2 * units), BF),
    ] + [((planes, rows, width), F32 if j == 0 else BF) for j in range(PLANE)]
    gate_shape = jax.ShapeDtypeStruct((flat_rows, 128), F32)

    def body(
        chosen_ref, gates_ref, piece_0, piece_1, piece_2, piece_3, out_hbm, shared_gu_hbm, shared_down_hbm,
        gu_hbm, down_hbm, router_hbm, both_hbm,
        grad_gate_ref, slots_hbm, grad_gu_hbm, grad_shared_hbm, total_0, total_1, total_2, total_3,
        rows_ref, out_ref, shared_gu_ref, shared_down_ref, gu_ref, down_ref, router_ref, both_ref,
        slots_ref, grad_gu_ref, grad_shared_ref, sum_0, sum_1, sum_2, sum_3, semaphores,
    ):
        copies = Copies(semaphores)
        totals, sums = (total_0, total_1, total_2, total_3), (sum_0, sum_1, sum_2, sum_3)
        coming = []
        for j, piece in enumerate((piece_0, piece_1, piece_2, piece_3)):
            for k in range(planes):
                target = rows_ref.at[pl.ds((j * planes + k) * rows, rows), :]
                coming.append(copies.start(piece.at[k], target))
        out_in = copies.start_rows(out_hbm, out_ref)
        shared_in = copies.start(shared_gu_hbm, shared_gu_ref)
        shared_in += copies.start(shared_down_hbm, shared_down_ref)
        down_in = copies.start_rows(down_hbm, down_ref)
        down_in += copies.start(gu_hbm, gu_ref)
        both_in = copies.start_rows(both_hbm, both_ref)
        both_in += copies.start_rows(router_hbm, router_ref)
        wait(out_in)
        for block in range(blocks):
            wait(coming[block])
            span = slice(block * rows, (block + 1) * rows)
            part = slice(block * capacity, (block + 1) * capacity)
            values = rows_ref[span, :].astype(F32)
            slots_ref[part, :] = dot_plain(
                chosen_ref[block], (gates_ref[span, 0:1] * values).astype(BF)
            ).astype(BF)
            picked = dot_first(chosen_ref[block], out_ref[part, :])
            own = jnp.sum(values * picked, axis=1, keepdims=True)
            grad_gate_ref[span, :] = jnp.broadcast_to(own, (rows, 128))
        leaving = copies.start(slots_ref, slots_hbm)
        wait(shared_in)
        grad_gate, grad_up = swiglu_parts(
            shared_gu_ref[:, :units].astype(F32),
            shared_gu_ref[:, units:].astype(F32),
            dot_last(rows_ref[...], shared_down_ref[...]),
        )
        grad_shared_ref[:, :units] = grad_gate
        grad_shared_ref[:, units:] = grad_up
        leaving += copies.start(grad_shared_ref, grad_shared_hbm)
        wait(down_in)
        for span in spans(hidden, TILE):
            above = slice(hidden + span.start, hidden + span.stop)
            grad_gate, grad_up = swiglu_parts(
                gu_ref[:, span].astype(F32),
                gu_ref[:, above].astype(F32),
                dot_last(slots_ref[...], down_ref[span, :]),
            )
            grad_gu_ref[:, span] = grad_gate
            grad_gu_ref[:, above] = grad_up
        leaving += copies.start(grad_gu_ref, grad_gu_hbm)
        wait(both_in)
        for strip in strips:
            grad_in = dot_last(grad_gu_ref[...], both_ref[strip, :]).astype(BF)
            shared = dot_last(grad_shared_ref[...], router_ref[strip, : 2 * units])
            for j in range(PLANE):
                for k in range(planes):
                    block = j * planes + k
                    moved = dot_first(
                        chosen_ref[block], grad_in[block * capacity : (block + 1) * capacity, :]
                    )
                    sums[j][k, :, strip] = (moved + shared[block * rows : (block + 1) * rows, :]).astype(
                        sums[j].dtype
                    )
                place = pl.ds(strip.start, strip.stop - strip.start)
                leaving += copies.start(sums[j].at[:, :, place], totals[j].at[:, :, place])
        wait(leaving)

    anywhere = pl.BlockSpec(memory_space=pl.ANY)
    moved = [out, shared_gu, shared_down, gu, down, shared_router, both]
    scratch = [pltpu.VMEM((flat_rows, width), BF)]
    scratch += [pltpu.VMEM(array.shape, BF) for array in moved]
    scratch += [pltpu.VMEM(*shape) for shape in shapes]
    count = blocks + 4 * PARTS + 3 + 3 + PLANE * len(strips)
    return pl.pallas_call(
        body,
        in_specs=[pl.BlockSpec(memory_space=pltpu.VMEM)] * 2 + [anywhere] * (PLANE + len(moved)),
        out_specs=[pl.BlockSpec(memory_space=pltpu.VMEM)] + [anywhere] * len(shapes),
        out_shape=[gate_shape] + [jax.ShapeDtypeStruct(*shape) for shape in shapes],
        scratch_shapes=scratch + [pltpu.SemaphoreType.DMA((count,))],
        compiler_params=pltpu.CompilerParams(vmem_limit_bytes=ROOM),
        cost_estimate=pl.CostEstimate(
            flops=2 * width * (3 * slots * hidden + flat_rows * 4 * units),
            bytes_accessed=2 * width * (3 * hidden + 4 * units + 6 * flat_rows) + 12 * slots * hidden,
            transcendentals=slots * hidden,
        ),
    )(chosen, gates, *pieces, *moved)


def turn(values, cosine, sine_table):
    lane = lax.broadcasted_iota(jnp.int32, values.shape, 1)
    wide = values.shape[1]
    swapped = jnp.where(
        lane % DR < DR // 2,
        pltpu.roll(values, wide - DR // 2, 1),
        pltpu.roll(values, DR // 2, 1),
    )
    return values * cosine + swapped * sine_table


def head_lanes(values, head):
    lane = lax.broadcasted_iota(jnp.int32, values.shape, 1)
    return jnp.where(lane // DR == head, values, jnp.zeros_like(values))


def attend(near, away, gain, down, latent_gain, query, up, heads, cosine, sine_table, place, places, early):
    sequences, rows, width = near.shape
    length = 2 * rows
    nope = heads * DN
    span = KVR + 2 * DR
    scaling = (DN + DR) ** (-0.5)

    def body(
        near_ref, away_ref, gain_ref, down_ref, latent_gain_ref, query_ref, up_ref, cos_ref, sin_ref, place_ref, places_ref, early_ref,
        normed_ref, latent_ref, compressed_ref, queries_ref, rope_ref, keyval_ref,
        attention_ref, context_ref,
    ):
        for side, ref in enumerate((near_ref, away_ref)):
            values = ref[0].astype(F32)
            normed_ref[side * rows : (side + 1) * rows, :] = rms_norm(values, gain_ref[...]).astype(BF)
        normed = normed_ref[...]
        latent = dot_plain(normed, down_ref[:, :span])
        latent_ref[...] = latent
        compressed = rms_norm(latent[:, :KVR], latent_gain_ref[...]).astype(BF)
        compressed_ref[...] = compressed
        key_rope = head_lanes(turn(latent[:, KVR:], cos_ref[...], sin_ref[...]), 0)
        key_rope = (key_rope + pltpu.roll(key_rope, DR, 1)).astype(BF)
        rope_ref[...] = key_rope
        query_raw = dot_plain(normed, query_ref[...])
        queries_ref[:, :nope] = query_raw[:, :nope].astype(BF)
        query_rope = turn(query_raw[:, nope:], cos_ref[...], sin_ref[...]).astype(BF)
        queries_ref[:, nope:] = query_rope
        keyval_ref[...] = dot_plain(compressed, up_ref[...]).astype(BF)
        visible = (places_ref[0:1, :] <= place_ref[:, 0:1]) | (early_ref[0, 0:1, :] > 0.0)
        for head in range(heads):
            start = head * (DN + DV)
            scores = dot_last(
                queries_ref[:, head * DN : (head + 1) * DN], keyval_ref[:, start : start + DN]
            ) + dot_last(head_lanes(query_rope, head), key_rope)
            scores = jnp.where(visible, scores * scaling, -1e30)
            weights = jnp.exp(scores - jnp.max(scores, axis=1, keepdims=True))
            attention = weights / jnp.sum(weights, axis=1, keepdims=True)
            attention_ref[0, head] = attention
            context_ref[:, head * DV : (head + 1) * DV] = dot_plain(
                attention.astype(BF), keyval_ref[:, start + DN : start + DN + DV]
            ).astype(BF)

    def by_rows(columns):
        return pl.BlockSpec((length, columns), lambda s: (s, 0))

    def halves():
        return pl.BlockSpec((1, rows, width), lambda s: (s, 0, 0))

    every = sequences * length
    fixed = (gain, down, latent_gain, query, up, cosine, sine_table, place, places)
    columns = (width, span, KVR, query.shape[1], 2 * DR, up.shape[1])
    kinds = (BF, F32, BF, BF, BF, BF)
    return pl.pallas_call(
        body,
        grid=(sequences,),
        in_specs=[halves(), halves()]
        + [whole(array) for array in fixed]
        + [pl.BlockSpec((1,) + early.shape[1:], lambda s: (s, 0, 0))],
        out_specs=[by_rows(c) for c in columns]
        + [
            pl.BlockSpec((1, heads, length, length), lambda s: (s, 0, 0, 0)),
            by_rows(heads * DV),
        ],
        out_shape=[jax.ShapeDtypeStruct((every, c), k) for c, k in zip(columns, kinds)]
        + [
            jax.ShapeDtypeStruct((sequences, heads, length, length), F32),
            jax.ShapeDtypeStruct((every, heads * DV), BF),
        ],
        compiler_params=pltpu.CompilerParams(vmem_limit_bytes=ROOM),
        cost_estimate=pl.CostEstimate(
            flops=2 * every * (width * (span + query.shape[1]) + KVR * up.shape[1]),
            bytes_accessed=32 * 1024 * 1024,
            transcendentals=every * length * heads,
        ),
    )(near, away, *fixed, early)


def attend_back(
    near, away, out, queries, rope, keyval, attention, normed, compressed, query, up, cosine, sine_table
):
    sequences, rows, width = near.shape
    length = 2 * rows
    heads = out.shape[0] // DV
    nope = heads * DN
    span = KVR + 2 * DR
    scaling = (DN + DR) ** (-0.5)

    def body(
        near_ref, away_ref, queries_ref, rope_ref, keyval_ref, attention_ref,
        normed_ref, compressed_ref, out_ref, query_ref, up_ref, cos_ref, sin_ref,
        grad_query_out, grad_up_out, own_ref, given_ref,
        grad_query_ref, grad_up_ref, incoming_ref, columns_ref, pairs_ref,
    ):
        @pl.when(pl.program_id(0) == 0)
        def _():
            grad_query_ref[...] = jnp.zeros_like(grad_query_ref)
            grad_up_ref[...] = jnp.zeros_like(grad_up_ref)

        incoming_ref[:rows, :] = near_ref[0]
        incoming_ref[rows:, :] = away_ref[0]
        incoming = incoming_ref[...]
        grad_context = dot_last(incoming, out_ref[...]).astype(BF)
        key_rope = rope_ref[...]
        query_rope = queries_ref[:, nope:]
        grad_query_rope = jnp.zeros((length, 2 * DR), F32)
        grad_key_rope = jnp.zeros((length, 2 * DR), F32)
        for head in range(heads):
            start = head * (DN + DV)
            attention = attention_ref[0, head]
            grad_head = grad_context[:, head * DV : (head + 1) * DV]
            grad_attention = dot_last(grad_head, keyval_ref[:, start + DN : start + DN + DV])
            grad_scores = attention * (
                grad_attention - jnp.sum(attention * grad_attention, axis=1, keepdims=True)
            )
            grad_scores = grad_scores.astype(BF)
            columns_ref[:, head * DN : (head + 1) * DN] = (
                dot_plain(grad_scores, keyval_ref[:, start : start + DN]) * scaling
            ).astype(BF)
            grad_query_rope += head_lanes(dot_plain(grad_scores, key_rope) * scaling, head)
            pairs_ref[:, start : start + DN] = (
                dot_first(grad_scores, queries_ref[:, head * DN : (head + 1) * DN]) * scaling
            ).astype(BF)
            pairs_ref[:, start + DN : start + DN + DV] = dot_first(
                attention.astype(BF), grad_head
            ).astype(BF)
            grad_key_rope += dot_first(grad_scores, head_lanes(query_rope, head)) * scaling
        columns_ref[:, nope:] = turn(grad_query_rope, cos_ref[...], -sin_ref[...]).astype(BF)
        grad_key_rope += pltpu.roll(grad_key_rope, DR, 1)
        columns = columns_ref[...]
        pairs = pairs_ref[...]
        grad_query_ref[...] += dot_first(normed_ref[...], columns)
        grad_up_ref[...] += dot_first(compressed_ref[...], pairs)
        latent = dot_last(pairs, up_ref[...])
        total = dot_last(columns, query_ref[...])
        own_ref[0, :, :width] = total[:rows].astype(BF)
        given_ref[0, :, :width] = total[rows:].astype(BF)
        own_ref[0, :, width : width + KVR] = latent[:rows].astype(BF)
        given_ref[0, :, width : width + KVR] = latent[rows:].astype(BF)
        own_ref[0, :, width + KVR :] = grad_key_rope[:rows].astype(BF)

        @pl.when(pl.program_id(0) == sequences - 1)
        def _():
            grad_query_out[...] = grad_query_ref[...].astype(BF)
            grad_up_out[...] = grad_up_ref[...].astype(BF)

        given_ref[0, :, width + KVR :] = grad_key_rope[rows:].astype(BF)

    def by_rows(columns):
        return pl.BlockSpec((length, columns), lambda s: (s, 0))

    def halves(columns):
        return pl.BlockSpec((1, rows, columns), lambda s: (s, 0, 0))

    every = sequences * length
    moving = (queries, rope, keyval)
    fixed = (out, query, up, cosine, sine_table)
    shapes = (
        (query.shape, BF), (up.shape, BF),
        ((sequences, rows, width + span), BF), ((sequences, rows, width + span), BF),
    )
    return pl.pallas_call(
        body,
        grid=(sequences,),
        in_specs=[halves(width), halves(width)]
        + [by_rows(array.shape[1]) for array in moving]
        + [pl.BlockSpec((1, heads, length, length), lambda s: (s, 0, 0, 0))]
        + [by_rows(normed.shape[1]), by_rows(compressed.shape[1])]
        + [whole(array) for array in fixed],
        out_specs=[whole(query), whole(up)]
        + [halves(width + span), halves(width + span)],
        out_shape=[jax.ShapeDtypeStruct(shape, kind) for shape, kind in shapes],
        scratch_shapes=[
            pltpu.VMEM(query.shape, F32),
            pltpu.VMEM(up.shape, F32),
            pltpu.VMEM((length, width), BF),
            pltpu.VMEM((length, query.shape[1]), BF),
            pltpu.VMEM((length, up.shape[1]), BF),
        ],
        compiler_params=pltpu.CompilerParams(vmem_limit_bytes=ROOM),
        cost_estimate=pl.CostEstimate(
            flops=4 * every * (width * (query.shape[1] + heads * DV) + KVR * up.shape[1]),
            bytes_accessed=48 * 1024 * 1024,
            transcendentals=0,
        ),
    )(near, away, *moving, attention, normed, compressed, *fixed)


def on_device(
    tokens,
    norm1_gain,
    q_weight,
    kv_down,
    latent_gain,
    kv_up,
    o_weight,
    norm2_gain,
    router,
    shared_gate_up,
    shared_down,
    expert_gate_up,
    expert_down,
    teacher,
    routes,
    prefix,
    token_count,
):
    cores = lax.axis_size("fsdp")
    depth = lax.axis_size("z")
    experts = depth * PLANE
    group = cores * PLANE
    heads = NH // group
    core = lax.axis_index("fsdp")
    plane_index = lax.axis_index("z")
    spot = lax.axis_index("r")
    own_expert = plane_index * PLANE + spot
    token_rows = tokens.shape[1]
    model_width = tokens.shape[2]
    seq_length = token_rows * cores
    capacity = -(-max(2, token_rows * TOP * 5 // (experts * 3)) // 16) * 16
    weight_rows = q_weight.shape[0]
    latent_rows = kv_up.shape[0]
    wide_q = heads * (DN + DR)
    wide_kv = heads * (DN + DV)
    scaling = (DN + DR) ** (-0.5)
    devices = cores * experts
    every = PLANE * seq_length
    everywhere = jnp.arange(devices, dtype=jnp.int32) ^ (core * experts + own_expert)

    sub = depth // PLANE
    shard_moves = [
        (z * PLANE + r, ((z % sub) * PLANE + r) * PLANE + z // sub)
        for z in range(depth)
        for r in range(PLANE)
    ]

    moved_o = lax.ppermute(o_weight, ("z", "r"), shard_moves)
    first_rows = tokens[0]

    fold = weight_rows // latent_rows
    up_fold = wide_kv // fold
    up_packed = kv_up.reshape(latent_rows, group, fold, up_fold)
    up_packed = up_packed.swapaxes(1, 2).reshape(weight_rows, group, up_fold)
    by_head = q_weight.reshape(weight_rows, group, heads, DN + DR)
    packed = jnp.concatenate(
        [
            by_head[..., :DN].reshape(weight_rows, group, heads * DN),
            by_head[..., DN:].reshape(weight_rows, group, heads * DR),
            up_packed,
        ],
        axis=2,
    )
    packed = lax.all_to_all(
        packed.swapaxes(0, 1), ("fsdp", "r"), split_axis=0, concat_axis=0, tiled=True
    )
    packed = packed.reshape(cores, PLANE * weight_rows, wide_q + up_fold)

    own_mask = jnp.any(
        routes[0][:, :, None] == jnp.arange(experts, dtype=jnp.int32)[None, None, :], axis=1
    )
    small = jnp.concatenate(
        [
            kv_down,
            router,
            norm1_gain[:, None],
            norm2_gain[:, None],
            jnp.pad(latent_gain, (0, weight_rows - latent_rows))[:, None],
            jnp.broadcast_to(prefix.astype(BF)[None, :], (weight_rows, 1)),
            own_mask.astype(BF).reshape(weight_rows, -1),
        ],
        axis=1,
    )
    small_width = -(-small.shape[1] // 128) * 128
    small = jnp.pad(small, ((0, 0), (0, small_width - small.shape[1])))
    small = jnp.stack([small] + [hop(small, "z", k) for k in range(1, depth)], axis=0)
    shared_both = shared_gate_up.reshape(weight_rows, 2 * cores, experts, shared_down.shape[0])
    shared_both = shared_both.transpose(2, 0, 1, 3).reshape(experts, weight_rows, -1)
    near_rows = jnp.stack(gather_plane(first_rows), axis=0)
    packed, small, near_rows, shared_both = stage(packed, small, near_rows, shared_both)
    packed = gather_columns(packed)
    away_rows = hop(near_rows, "fsdp", 1)
    small = jnp.stack(gather_plane(small), axis=1)
    small = jnp.stack([small, hop(small, "fsdp", 1)], axis=0)
    shared_both = swap_plane(after(shared_both, small))
    packed, shared_both, moved_o = stage(packed, shared_both, moved_o, small, away_rows)[:3]
    output_weight = gather_columns_apart(moved_o).reshape(heads * DV, model_width)
    small = small.reshape(devices, weight_rows, small_width)
    prefixes = small[:PLANE, 0, KVR + DR + experts + 3].astype(F32)
    masks = small[:experts, :, KVR + DR + experts + 4 :][:, :, : token_rows * experts // weight_rows]
    masks = masks.astype(F32).reshape(experts, token_rows, experts)
    small = jnp.take(small, everywhere, axis=0, mode="clip").reshape(model_width, small_width)
    down_weight = small[:, : KVR + DR]
    router_weight = small[:, KVR + DR : KVR + DR + experts]
    gains = small[:, KVR + DR + experts : KVR + DR + experts + 3].astype(F32).T
    gain_one_f = gains[0]
    gain_two_f = gains[1]
    latent_gain_f = gains[2].reshape(-1, weight_rows)[:, :latent_rows].reshape(KVR)

    half = jnp.arange(token_rows, dtype=jnp.int32)
    position = jnp.concatenate([core * token_rows + half, (1 - core) * token_rows + half])
    cosine, sine_table = tables(position, DR)
    spread_cos = jnp.tile(cosine, (1, 4))
    spread_sin = jnp.tile(jnp.concatenate([-sine_table, sine_table], axis=1), (1, 2))
    places = position.astype(F32)
    early = (places[None, :] < prefixes[:, None]).astype(F32)
    early = jnp.broadcast_to(early[:, None, :], (PLANE, 8, seq_length))
    packed = packed.swapaxes(0, 1).reshape(model_width, wide_q + up_fold)
    query_weight = packed[:, :wide_q]
    up_weight = packed[:, wide_q:].reshape(KVR, fold * up_fold)


    normed, latent, compressed, queries, key_rope, keyval, attention, context = attend(
        near_rows, away_rows, gain_one_f[None], small, latent_gain_f[None], query_weight,
        up_weight, heads, spread_cos, spread_sin,
        jnp.broadcast_to(places[:, None], (seq_length, 128)),
        jnp.broadcast_to(places[None, :], (8, seq_length)), early,
    )
    expert_both_weight = lax.all_gather(expert_gate_up, "fsdp", axis=1, tiled=True)[0]
    expert_down_weight = lax.all_gather(expert_down, "fsdp", axis=2, tiled=True)[0]
    unit = shared_down.shape[0]
    shared_units = cores * unit
    masks = after(masks, packed)
    order = jnp.arange(experts, dtype=jnp.int32) ^ own_expert
    mine = (jnp.arange(experts, dtype=jnp.int32) == own_expert).astype(F32)
    taken = jnp.sum(masks * mine[None, None, :], axis=2)
    rank = jnp.cumsum(taken, axis=1) - taken
    select = taken[:, None, :] * (
        rank[:, None, :] == jnp.arange(capacity, dtype=F32)[None, :, None]
    ).astype(F32)
    select_low = select.astype(BF)
    steps = depth
    lots = [[k] for k in range(depth)]
    lots = lots[:1] + lots[2:] + lots[1:2]
    block_order = np.array(
        [k * PLANE + j for planes in lots for j in range(PLANE) for k in planes], dtype=np.int32
    )
    chunk_select = jnp.take(select_low, block_order, axis=0, mode="clip")
    chunk_select = chunk_select.reshape(steps, PLANE, capacity, token_rows)
    chunk_masks = jnp.take(masks, block_order, axis=0, mode="clip")
    chunk_masks = chunk_masks.reshape(steps, PLANE * token_rows, experts)
    context, output_weight, chunk_select, chunk_masks = stage(
        context, output_weight, chunk_select, chunk_masks
    )
    sides = context.reshape(PLANE, cores, token_rows, heads * DV)

    def project(side):
        flat = sides[:, side].reshape(PLANE * token_rows, heads * DV)
        return dot_plain(flat, output_weight).reshape(PLANE, token_rows, model_width)

    given_part = hop(project(1).astype(BF), "fsdp", 1)
    own_part = project(0).astype(BF)
    shared_down_weight = both_cores(shared_down)
    own_part, given_part, shared_both, shared_down_weight = stage(
        own_part, given_part, shared_both, shared_down_weight
    )
    shared_both = swap_column(shared_both).reshape(experts * weight_rows, 2 * shared_units)
    own_rows = tokens[0].astype(F32)
    hidden = own_rows + scatter_sides(own_part, given_part)
    hidden, shared_both = stage(hidden, shared_both)
    shared_both_weight = both_cores(shared_both)
    normed2 = rms_norm(hidden, gain_two_f).astype(BF)

    def gates_of(logits, mask):
        logits = jnp.where(mask, logits, -1e30)
        odds = jnp.where(mask, jnp.exp(logits - jnp.max(logits, axis=-1, keepdims=True)), 0.0)
        return odds / jnp.sum(odds, axis=-1, keepdims=True)

    own_gates = gates_of(dot_plain(normed2, router_weight), own_mask)
    wide_unit = -(-unit // 128) * 128
    padded = cores * wide_unit

    def pad_columns(values, columns):
        return jnp.pad(values, ((0, 0), (0, columns - values.shape[1])))

    shared_router = jnp.concatenate(
        [
            pad_columns(shared_both_weight[:, start : start + unit], wide_unit)
            for start in range(0, 2 * shared_units, unit)
        ]
        + [
            pad_columns(router_weight, -(-experts // 128) * 128),
        ],
        axis=1,
    )
    shared_rows = jnp.pad(
        shared_down_weight.reshape(cores, unit, model_width),
        ((0, 0), (0, wide_unit - unit), (0, 0)),
    ).reshape(padded, model_width)

    def passes(values, compute, besides):
        def fetch(values, number):
            return jnp.stack([hop(values, "z", k) if k else values for k in lots[number]], axis=0)

        source, pieces, totals, summed = fetch(values, 0), None, None, None
        returned, results = [], []
        for step in range(steps + 3):
            later = [values, None, None, None, None, None]
            if step + 1 < steps:
                later[1] = fetch(values, step + 1)
            if pieces is not None:
                later[3] = compute(step - 1, pieces, results)
            if source is not None and totals is not None:
                count, half = source.shape[0], source.shape[1] // 2
                along, across = [
                    hop(jnp.concatenate([source, totals[j]], axis=0), "r", j) for j in (1, 2)
                ]
                opposite = hop(totals[3], "r", 3)
                behind = later[3][1]
                far = jnp.concatenate(
                    [
                        hop(after(along[:count, :half], behind), "r", 2),
                        hop(after(across[:count, half:], behind), "r", 1),
                    ],
                    axis=1,
                )
                later[2] = [source, along[:count], across[:count], far]
                later[4] = totals[0] + sum(
                    part.astype(F32) for part in (along[count:], across[count:], opposite)
                )
            elif source is not None:
                later[2] = gather_plane(source)
            elif totals is not None:
                later[4] = scatter_plane(totals)
            if summed is not None:
                later[5] = [
                    hop(summed[i].astype(BF), "z", k) if k else summed[i]
                    for i, k in enumerate(lots[step - 3])
                ]
            later.append(besides(step, summed if totals is None else totals[0], results))
            values, source, pieces, totals, summed, back, beside = lax.optimization_barrier(later)
            if beside is not None:
                results.append(beside)
            if back is not None:
                returned += [part.astype(F32) for part in back]
        return sum(returned), results

    def forward_chunk(number, pieces, results):
        values = expert_forward(
            pieces, chunk_select[number], chunk_masks[number], mine[None], results[0][0],
            expert_both_weight, expert_down_weight, results[0][1],
        )
        arrived.append([piece.reshape(-1, model_width) for piece in pieces])
        saved.append(values[:7])
        return list(values[7:])

    def backward_chunk(number, pieces, results):
        gates, expert_in, expert_gu, expert_act, expert_out, shared_gu, shared_act = saved[number]
        values = expert_backward(
            pieces, chunk_select[number], gates, expert_gu, expert_out, shared_gu, shared_router,
            expert_both_weight, expert_down_weight, shared_rows,
        )
        grad_arrived.append([piece.reshape(-1, model_width) for piece in pieces])
        grads.append(values[:4])
        return list(values[4:])

    arrived, saved, grad_arrived, grads = [], [], [], []
    routed, results = passes(
        normed2,
        forward_chunk,
        lambda step, behind, results: (shared_router, shared_rows, chunk_select, chunk_masks)
        if step == 0
        else None,
    )
    shared_router, shared_rows = results[0][:2]
    output = hidden + routed
    misfit = output - teacher[0].astype(F32)
    misfit_low = misfit.astype(BF)

    def products(lefts, rights, behind, tall, wide=None):
        return sums_of_products([after(lefts[0], behind)] + lefts[1:], rights, tall, wide)

    def kept(lists, entry):
        return [values[entry] for values in lists]

    def joined(lists):
        return [piece for pieces in lists for piece in pieces]

    def weight_grads(step, behind, results):
        if step == steps + 1:
            grad_gate = jnp.concatenate([values[0][:, 0] for values in grads], axis=0)
            grad_gate = jnp.take(
                after(grad_gate.reshape(experts, token_rows), behind),
                np.argsort(block_order), axis=0, mode="clip",
            )
            squares = jnp.broadcast_to(jnp.sum(misfit * misfit)[None, None], (experts, 128))
            notes = jnp.concatenate([jnp.take(grad_gate, order, axis=0, mode="clip"), squares], axis=1)
            return (
                products(joined(arrived), kept(grads, 3), behind, 512),
                products(kept(saved, 6), joined(grad_arrived), behind, padded, 512),
                notes,
            )
        if step == steps + 2:
            notes = lax.all_to_all(results[0][2], ("z", "r"), split_axis=0, concat_axis=0, tiled=True)
            return products(kept(saved, 3), kept(grads, 1), behind, FFE, 512), notes
        return None

    grad_returned, results = passes(misfit_low, backward_chunk, weight_grads)
    grad_shared, (grad_expert_down, notes) = results
    grad_shared_both, grad_shared_down = grad_shared[:2]
    grad_expert_down = lax.psum_scatter(
        grad_expert_down[None], "fsdp", scatter_dimension=2, tiled=True
    )
    grad_shared_down = lax.psum_scatter(
        grad_shared_down, "fsdp", scatter_dimension=0, tiled=True
    )[:unit]
    grad_shared_both = lax.psum_scatter(
        grad_shared_both, "fsdp", scatter_dimension=0, tiled=True
    )
    grad_shared_both = jnp.concatenate(
        [
            grad_shared_both[:, start : start + unit].astype(BF)
            for start in range(0, 2 * padded, wide_unit)
        ],
        axis=1,
    )
    grad_shared_both = lax.all_to_all(
        grad_shared_both.reshape(experts, weight_rows, 2 * shared_units),
        ("z", "r"),
        split_axis=0,
        concat_axis=0,
        tiled=True,
    )

    grad_gates = notes[:, :token_rows].T
    all_squares = jnp.sum(notes[:, token_rows])[None]
    all_squares = all_squares + hop(jnp.broadcast_to(all_squares, (8, 128)), "fsdp", 1)[0, :1]
    loss_value = all_squares / (token_count.astype(F32) * model_width)
    grad_logits = (
        own_gates * (grad_gates - jnp.sum(own_gates * grad_gates, axis=1, keepdims=True))
    ).astype(BF)
    grad_normed2 = grad_returned + dot_last(grad_logits, router_weight)
    grad_hidden_norm, grad_gain_two = norm_back(hidden, gain_two_f, grad_normed2)
    grad_hidden = misfit + grad_hidden_norm
    near_grad = jnp.stack(gather_plane(grad_hidden.astype(BF)), axis=0)
    grad_expert_gate_up = products(kept(saved, 1), kept(grads, 2), grad_hidden, 256)
    near_grad, grad_expert_gate_up, grad_shared_both = stage(
        near_grad, grad_expert_gate_up, grad_shared_both
    )
    grad_expert_gate_up = lax.psum_scatter(
        grad_expert_gate_up[None], "fsdp", scatter_dimension=1, tiled=True
    )
    away_grad = hop(near_grad, "fsdp", 1)
    flat = (PLANE * token_rows, model_width)
    grad_output_weight = sums_of_products(
        [sides[:, 0].reshape(flat[0], -1), sides[:, 1].reshape(flat[0], -1)],
        [near_grad.reshape(flat), away_grad.reshape(flat)],
        heads * DV,
        512,
        BF,
    )
    grad_output_weight = by_column(grad_output_weight.reshape(depth, weight_rows, model_width))
    grad_router = dot_first(normed2, grad_logits)
    grad_output_weight, away_grad, grad_router = stage(grad_output_weight, away_grad, grad_router)
    grad_output_weight = sum_columns(grad_output_weight).astype(BF)
    grad_query_weight, grad_up, own_part, given_part = attend_back(
        near_grad, away_grad, output_weight, queries, key_rope, keyval, attention,
        normed, compressed, query_weight, up_weight, spread_cos, spread_sin,
    )
    grad_query_weight, grad_up, own_part, given_part, grad_output_weight = stage(
        grad_query_weight, grad_up, own_part, given_part, grad_output_weight
    )
    grad_packed = jnp.concatenate([grad_query_weight, grad_up.reshape(model_width, up_fold)], axis=1)
    grad_packed = grad_packed.reshape(cores, depth, PLANE * weight_rows, wide_q + up_fold)
    grad_packed = grad_packed.swapaxes(0, 1)
    given_part = hop(given_part, "fsdp", 1)
    own_part, given_part, grad_packed = stage(own_part, given_part, grad_packed)
    grad_packed = lax.all_to_all(grad_packed, "z", split_axis=0, concat_axis=0, tiled=True)
    normed_sum = scatter_sides(own_part, given_part)
    latent_sum = normed_sum[:, model_width:]
    own_latent = latent[:token_rows]
    grad_latent_norm, grad_latent_gain = norm_back(
        own_latent[:, :KVR], latent_gain_f, latent_sum[:, :KVR]
    )
    grad_latent = jnp.concatenate(
        [
            grad_latent_norm,
            unrotate(latent_sum[:, KVR : KVR + DR], cosine[:token_rows], sine_table[:token_rows]),
        ],
        axis=1,
    ).astype(BF)
    own_normed = normed[:token_rows]
    grad_normed = normed_sum[:, :model_width] + dot_last(grad_latent, down_weight)
    grad_flat_norm, grad_gain_one = norm_back(own_rows, gain_one_f, grad_normed)
    grad_tokens = grad_hidden + grad_flat_norm
    grad_latent_gain = jnp.pad(
        grad_latent_gain.reshape(-1, latent_rows), ((0, 0), (0, weight_rows - latent_rows))
    ).reshape(model_width)
    base = KVR + DR + experts
    columns = jnp.arange(small_width, dtype=jnp.int32)[None, :]

    def widen(values, start):
        return jnp.pad(values, ((0, 0), (start, small_width - start - values.shape[1])))

    grad_small = (
        dot_first(own_normed, widen(grad_latent, 0))
        + widen(grad_router, KVR + DR)
        + jnp.where(columns == base, grad_gain_one[:, None], 0.0)
        + jnp.where(columns == base + 1, grad_gain_two[:, None], 0.0)
        + jnp.where(columns == base + 2, grad_latent_gain[:, None], 0.0)
    )
    grad_small = straight(grad_small.astype(BF)).reshape(devices, weight_rows, small_width)
    grad_small = jnp.take(grad_small, everywhere, axis=0, mode="clip")
    grad_small = grad_small.reshape(cores, depth, PLANE, weight_rows, small_width)
    grad_tail = grad_small[0].astype(F32) + hop(grad_small[1], "fsdp", 1).astype(F32)
    grad_tail, grad_packed, grad_output_weight = stage(
        straight(grad_tail.astype(BF)), grad_packed, grad_output_weight
    )
    grad_packed = jnp.sum(grad_packed.astype(F32), axis=0).astype(BF)
    grad_shared_gate_up = (
        after(grad_shared_both, grad_tail)
        .reshape(experts, weight_rows, 2 * cores, unit)
        .transpose(1, 2, 0, 3)
        .reshape(weight_rows, 2 * FFS)
        .astype(F32)
    )
    grad_packed = lax.all_to_all(
        grad_packed.reshape(group, weight_rows, wide_q + up_fold),
        ("fsdp", "r"),
        split_axis=0,
        concat_axis=0,
        tiled=True,
    )
    grad_small = scatter_plane([grad_tail[:, j] for j in range(PLANE)])
    grad_output_weight = lax.ppermute(
        grad_output_weight, ("z", "r"), [(b, a) for a, b in shard_moves]
    )
    grad_small, grad_packed, grad_output_weight = stage(
        grad_small, grad_packed, grad_output_weight
    )
    grad_output_weight = grad_output_weight.astype(F32)
    grad_packed = grad_packed.swapaxes(0, 1)
    grad_small = grad_small[0] + sum(
        hop(grad_small[k].astype(BF), "z", k).astype(F32) for k in range(1, depth)
    )
    grad_q_weight = jnp.concatenate(
        [
            grad_packed[:, :, : heads * DN].reshape(weight_rows, group, heads, DN),
            grad_packed[:, :, heads * DN : wide_q].reshape(weight_rows, group, heads, DR),
        ],
        axis=3,
    )
    grad_q_weight = grad_q_weight.reshape(weight_rows, -1).astype(F32)
    grad_kv_up = (
        grad_packed[:, :, wide_q:]
        .reshape(latent_rows, fold, group, up_fold)
        .swapaxes(1, 2)
        .reshape(latent_rows, -1)
        .astype(F32)
    )
    return (
        output.astype(BF)[None],
        loss_value,
        grad_tokens[None],
        grad_small[:, base],
        grad_q_weight,
        grad_small[:, : KVR + DR],
        grad_small[:latent_rows, base + 2],
        grad_kv_up,
        grad_output_weight,
        grad_small[:, base + 1],
        grad_small[:, KVR + DR : base],
        grad_shared_gate_up,
        grad_shared_down,
        grad_expert_gate_up,
        grad_expert_down,
    )


def solution(mesh):
    cores = mesh.shape["fsdp"]
    experts = mesh.shape["expert"]
    grid = Mesh(mesh.devices.reshape(cores, experts // PLANE, PLANE), ("fsdp", "z", "r"))
    expert = ("z", "r")
    every = ("fsdp", "z", "r")
    return jax.shard_map(
        on_device,
        mesh=grid,
        in_specs=(
            P(expert, "fsdp", None),
            P(every),
            P(every, None),
            P(every, None),
            P(every),
            P(every, None),
            P(every, None),
            P(every),
            P(every, None),
            P(every, None),
            P(every, None),
            P(expert, "fsdp", None),
            P(expert, None, "fsdp"),
            P(expert, "fsdp", None),
            P(expert, "fsdp", None),
            P(expert),
            P(),
        ),
        out_specs=(
            P(expert, "fsdp", None),
            P(),
            P(expert, "fsdp", None),
            P(every),
            P(every, None),
            P(every, None),
            P(every),
            P(every, None),
            P(every, None),
            P(every),
            P(every, None),
            P(every, None),
            P(every, None),
            P(expert, "fsdp", None),
            P(expert, None, "fsdp"),
        ),
        check_vma=False,
    )
```

profile of v0, /device:TPU:0, one launch (start us, length us, event | category | flops | bytes accessed | tf_op | source)
XLA Modules:
  0.0 846.2 jit_solution(17996777712805922312)
XLA Ops:
  8.2 2.9 collective-permute-start.3
  21.9 4.2 all-to-all-start
  31.1 3.6 collective-permute-start.14
  34.7 4.2 collective-permute-done.1
  40.0 3.4 pad_maximum_fusion.1.near_ref
  45.5 4.8 collective-permute-start.7
  53.0 8.1 all-to-all-start.1
  61.6 6.9 collective-permute-done.9
  92.8 3.4 collective-permute-start.13
  123.3 16.0 %shard_map.298 = (bf16[1024,2048]{1,0:T(8,128)(2,1)}, f32[1024,640]{1,0:T(8,128)}, bf16[1024,512]{1,0:T(8,128)(2,1)}, bf16[1024,384]{1,0:T(8,128)(2,1)}, bf16[10...) custom-call(bf16[4,128,2048]{2,1,0:T(8,128)(2,1)} %pad_maximum_fusion.1., ...), custom_call_target="tpu_custom_call" | custom-call | flops 4831838208 | bytes 33554432 | tf_op jit(solution)/shard_map/pallas_call | solution.py:521
  145.3 3.4 collective-permute-done.19
  152.8 3.8 collective-permute-start.25
  161.0 2.7 collective-permute-start.22
  167.2 6.4 collective-permute-done.24
  176.7 9.0 %collective-permute-done.21 = bf16[128,2048]{1,0:T(8,128)(2,1)} collective-permute-done((bf16[128,2048]{1,0:T(8,128)(2,1)}, bf16[128,2048]{1,0:T(8,128)(2,1)}, u32[]{:S(2)}, u32[]{:S(2)}) %collective-permute-start.21) | collective-permute-done | bytes 524320 | tf_op jit(solution)/shard_map/ppermute | solution.py:93
  198.2 20.9 %collective-permute-done.26 = bf16[128,2048]{1,0:T(8,128)(2,1)} collective-permute-done((bf16[128,2048]{1,0:T(8,128)(2,1)S(1)}, bf16[128,2048]{1,0:T(8,128)(2,1)}, u32[]{:S(2)}, u32[]{:S(2)}) %collective-permute-start.26) | collective-permute-done | bytes 524320 | tf_op jit(solution)/shard_map/ppermute | solution.py:93
  225.0 18.2 %shard_map.299 = (f32[512,128]{1,0:T(8,128)}, bf16[320,2048]{1,0:T(8,128)(2,1)}, bf16[320,2816]{1,0:T(8,128)(2,1)}, bf16[320,1408]{1,0:T(8,128)(2,1)}, bf16[320,...) custom-call(bf16[4,80,128]{2,1,0:T(8,128)(2,1)} %get-tuple-element.6, ...), custom_call_target="tpu_custom_call" | custom-call | flops 7683964928 | bytes 35291136 | tf_op jit(solution)/shard_map/pallas_call | solution.py:335
  251.8 18.3 %shard_map.300 = (f32[512,128]{1,0:T(8,128)}, bf16[320,2048]{1,0:T(8,128)(2,1)}, bf16[320,2816]{1,0:T(8,128)(2,1)}, bf16[320,1408]{1,0:T(8,128)(2,1)}, bf16[320,...) custom-call(bf16[4,80,128]{2,1,0:T(8,128)(2,1)} %get-tuple-element.6, ...), custom_call_target="tpu_custom_call" | custom-call | flops 7683964928 | bytes 35291136 | tf_op jit(solution)/shard_map/pallas_call | solution.py:335
  276.8 9.4 %collective-permute-done.40 = bf16[1,128,2048]{2,1,0:T(8,128)(2,1)} collective-permute-done((bf16[1,128,2048]{2,1,0:T(8,128)(2,1)}, bf16[1,128,2048]{2,1,0:T(8,128)(2,1)}, u32[]{:S(2)}, u32[]{:S(2)}) %collective-permute-start.40) | collective-permute-done | bytes 524320 | tf_op jit(solution)/shard_map/ppermute | solution.py:93
  294.9 18.6 %shard_map.301 = (f32[512,128]{1,0:T(8,128)}, bf16[320,2048]{1,0:T(8,128)(2,1)}, bf16[320,2816]{1,0:T(8,128)(2,1)}, bf16[320,1408]{1,0:T(8,128)(2,1)}, bf16[320,...) custom-call(bf16[4,80,128]{2,1,0:T(8,128)(2,1)} %get-tuple-element.6, ...), custom_call_target="tpu_custom_call" | custom-call | flops 7683964928 | bytes 35291136 | tf_op jit(solution)/shard_map/pallas_call | solution.py:335
  313.6 10.3 %collective-permute-done.42 = bf16[2,128,2048]{2,1,0:T(8,128)(2,1)S(1)} collective-permute-done((bf16[2,128,2048]{2,1,0:T(8,128)(2,1)}, bf16[2,128,2048]{2,1,0:T(8,128)(2,1)S(1)}, u32[]{:S(2)}, u32[]{:S(2)}) %collective-permute-start.42) | collective-permute-done | bytes 1048608 | tf_op jit(solution)/shard_map/ppermute | solution.py:93
  325.8 3.9 collective-permute-done.45
  337.9 18.2 %shard_map.302 = (f32[512,128]{1,0:T(8,128)}, bf16[320,2048]{1,0:T(8,128)(2,1)}, bf16[320,2816]{1,0:T(8,128)(2,1)}, bf16[320,1408]{1,0:T(8,128)(2,1)}, bf16[320,...) custom-call(bf16[4,80,128]{2,1,0:T(8,128)(2,1)} %get-tuple-element.6, ...), custom_call_target="tpu_custom_call" | custom-call | flops 7683964928 | bytes 35291136 | tf_op jit(solution)/shard_map/pallas_call | solution.py:335
  363.0 9.6 %collective-permute-done.50 = bf16[1,128,2048]{2,1,0:T(8,128)(2,1)S(1)} collective-permute-done((bf16[1,128,2048]{2,1,0:T(8,128)(2,1)S(1)}, bf16[1,128,2048]{2,1,0:T(8,128)(2,1)S(1)}, u32[]{:S(2)}, u32[]{:S(2)}) %collective-permute-start.50) | collective-permute-done | bytes 524320 | tf_op jit(solution)/shard_map/ppermute | solution.py:93
  372.6 11.0 %collective-permute-done.51 = bf16[1,128,2048]{2,1,0:T(8,128)(2,1)S(1)} collective-permute-done((bf16[1,128,2048]{2,1,0:T(8,128)(2,1)S(1)}, bf16[1,128,2048]{2,1,0:T(8,128)(2,1)S(1)}, u32[]{:S(2)}, u32[]{:S(2)}) %collective-permute-start.51) | collective-permute-done | bytes 524320 | tf_op jit(solution)/shard_map/ppermute | solution.py:93
  384.0 11.9 %collective-permute-done.54 = bf16[128,2048]{1,0:T(8,128)(2,1)S(1)} collective-permute-done((bf16[128,2048]{1,0:T(8,128)(2,1)S(1)}, bf16[128,2048]{1,0:T(8,128)(2,1)S(1)}, u32[]{:S(2)}, u32[]{:S(2)}) %collective-permute-start.54) | collective-permute-done | bytes 524320 | tf_op jit(solution)/shard_map/ppermute | solution.py:93
  402.3 8.3 collective-permute-done.57.piece_2
  410.6 4.7 collective-permute-done.56.piece_1
  415.3 8.5 %collective-permute-done.58.piece_3 = bf16[1,128,2048]{2,1,0:T(8,128)(2,1)S(1)} collective-permute-done((bf16[1,128,2048]{2,1,0:T(8,128)(2,1)}, bf16[1,128,2048]{2,1,0:T(8,128)(2,1)S(1)}, u32[]{:S(2)}, u32[]{:S(2)}) %collective-permute-start.58) | collective-permute-done | bytes 524320 | tf_op jit(solution)/shard_map/ppermute | solution.py:93
  429.9 18.1 %shard_map.303 = (f32[512,128]{1,0:T(8,128)}, bf16[320,2048]{1,0:T(8,128)(2,1)}, bf16[320,2816]{1,0:T(8,128)(2,1)}, bf16[512,512]{1,0:T(8,128)(2,1)}, f32[1,128,...) custom-call(bf16[4,80,128]{2,1,0:T(8,128)(2,1)} %get-tuple-element.6, ...), custom_call_target="tpu_custom_call" | custom-call | flops 7683964928 | bytes 39485440 | tf_op jit(solution)/shard_map/pallas_call | solution.py:438
  448.1 4.3 collective-permute-done.62.piece_3
  452.4 2.9 pad_maximum_fusion.9
  459.5 18.1 %shard_map.304 = (f32[512,128]{1,0:T(8,128)}, bf16[320,2048]{1,0:T(8,128)(2,1)}, bf16[320,2816]{1,0:T(8,128)(2,1)}, bf16[512,512]{1,0:T(8,128)(2,1)}, f32[1,128,...) custom-call(bf16[4,80,128]{2,1,0:T(8,128)(2,1)} %get-tuple-element.6, ...), custom_call_target="tpu_custom_call" | custom-call | flops 7683964928 | bytes 39485440 | tf_op jit(solution)/shard_map/pallas_call | solution.py:438
  477.7 3.4 collective-permute-done.65
  485.4 8.9 %collective-permute-done.68 = bf16[1,128,2048]{2,1,0:T(8,128)(2,1)S(1)} collective-permute-done((bf16[1,128,2048]{2,1,0:T(8,128)(2,1)}, bf16[1,128,2048]{2,1,0:T(8,128)(2,1)S(1)}, u32[]{:S(2)}, u32[]{:S(2)}) %collective-permute-start.68) | collective-permute-done | bytes 524320 | tf_op jit(solution)/shard_map/ppermute | solution.py:93
  503.2 18.1 %shard_map.305 = (f32[512,128]{1,0:T(8,128)}, bf16[320,2048]{1,0:T(8,128)(2,1)}, bf16[320,2816]{1,0:T(8,128)(2,1)}, bf16[512,512]{1,0:T(8,128)(2,1)}, f32[1,128,...) custom-call(bf16[4,80,128]{2,1,0:T(8,128)(2,1)} %get-tuple-element.6, ...), custom_call_target="tpu_custom_call" | custom-call | flops 7683964928 | bytes 39485440 | tf_op jit(solution)/shard_map/pallas_call | solution.py:438
  522.5 9.3 %collective-permute-done.70 = bf16[2,128,2048]{2,1,0:T(8,128)(2,1)S(1)} collective-permute-done((bf16[2,128,2048]{2,1,0:T(8,128)(2,1)}, bf16[2,128,2048]{2,1,0:T(8,128)(2,1)S(1)}, u32[]{:S(2)}, u32[]{:S(2)}) %collective-permute-start.70) | collective-permute-done | bytes 1048608 | tf_op jit(solution)/shard_map/ppermute | solution.py:93
  534.2 3.3 collective-permute-done.73
  545.9 18.1 %shard_map.306 = (f32[512,128]{1,0:T(8,128)}, bf16[320,2048]{1,0:T(8,128)(2,1)}, bf16[320,2816]{1,0:T(8,128)(2,1)}, bf16[512,512]{1,0:T(8,128)(2,1)}, f32[1,128,...) custom-call(bf16[4,80,128]{2,1,0:T(8,128)(2,1)} %get-tuple-element.6, ...), custom_call_target="tpu_custom_call" | custom-call | flops 7683964928 | bytes 39485440 | tf_op jit(solution)/shard_map/pallas_call | solution.py:438
  572.9 7.1 shard_map.308
  580.0 9.4 %shard_map.307 = f32[2048,512]{1,0:T(8,128)} custom-call(bf16[128,2048]{1,0:T(8,128)(2,1)} %bitcast.91.refs_0_, bf16[128,2048]{1,0:T(8,128)(2,1)} %bitcast.92.refs_1_, bf16[128,2048]{1,0:T(8,128)(2,1)} %bitcast.93.refs_2_, bf16[128,2048]{1,0:T(8,128)(2,1)} %bitcast.94.refs_3_, bf16[128,2048]{1,0:T(8,128)(2,1)} %bitcast.95.refs_4_, ...), custom_call_target="tpu_custom_call" | custom-call | flops 4294967296 | bytes 14680064 | tf_op jit(solution)/shard_map/pallas_call | solution.py:188
  591.3 2.7 add_add_fusion.1
  595.3 3.5 all-to-all-start.2
  600.8 13.5 %shard_map.309 = f32[1408,2048]{1,0:T(8,128)} custom-call(bf16[320,1408]{1,0:T(8,128)(2,1)} %get-tuple-element.431.refs_0_, bf16[320,1408]{1,0:T(8,128)(2,1)} %get-tuple-element.432.refs_1_, bf16[320,1408]{1,0:T(8,128)(2,1)} %get-tuple-element.433.refs_2_, bf16[320,1408]{1,0:T(8,128)(2,1)} %get-tuple-element.434.refs_3_, ...), custom_call_target="tpu_custom_call" | custom-call | flops 7381975040 | bytes 20381696 | tf_op jit(solution)/shard_map/pallas_call | solution.py:188
  616.7 3.3 multiply_reduce_fusion
  628.5 6.1 all-to-all-start.3
  634.7 24.4 %shard_map.310 = f32[2048,2816]{1,0:T(8,128)} custom-call(bf16[320,2048]{1,0:T(8,128)(2,1)} %get-tuple-element.446.refs_0_, bf16[320,2048]{1,0:T(8,128)(2,1)} %get-tuple-element.447.refs_1_, bf16[320,2048]{1,0:T(8,128)(2,1)} %get-tuple-element.448.refs_2_, bf16[320,2048]{1,0:T(8,128)(2,1)} %get-tuple-element.449.refs_3_, ...), custom_call_target="tpu_custom_call" | custom-call | flops 14763950080 | bytes 35520512 | tf_op jit(solution)/shard_map/pallas_call | solution.py:188
  669.1 5.7 shard_map.311
  681.3 20.7 %shard_map.312 = (bf16[2048,384]{1,0:T(8,128)(2,1)}, bf16[512,512]{1,0:T(8,128)(2,1)}, bf16[4,128,2688]{2,1,0:T(8,128)(2,1)}, bf16[4,128,2688]{2,1,0:T(8,128)(2,1)}) custom-call(bf16[4,128,2048]{2,1,0:T(8,128)(2,1)} %copy-done.2, bf16[4,128,2048]{2,1,0:T(8,128)(2,1)} %copy-done.18, bf16[1024,384]{1,0:T(8,128)(2,1)} %get-tuple-element.457.queries_ref, ...), custom_call_target="tpu_custom_call" | custom-call | flops 6442450944 | bytes 50331648 | tf_op jit(solution)/shard_map/pallas_call | solution.py:629
  723.6 4.7 all-to-all-start.4
  728.4 4.9 collective-permute-done.92
  733.3 15.1 %collective-permute-done.93 = bf16[128,2688]{1,0:T(8,128)(2,1)} collective-permute-done((bf16[128,2688]{1,0:T(8,128)(2,1)}, bf16[128,2688]{1,0:T(8,128)(2,1)}, u32[]{:S(2)}, u32[]{:S(2)}) %collective-permute-start.93) | collective-permute-done | bytes 688160 | tf_op jit(solution)/shard_map/ppermute | solution.py:93
  755.0 4.1 fusion.10
  759.1 4.3 add_convert_fusion.1
  763.4 2.9 gather_fusion.9
  777.7 2.9 reduce_sum.156
  780.6 4.3 all-to-all-start.5
  789.4 2.7 fusion.7
  792.2 3.6 collective-permute-start.99
  795.8 3.7 reshape.624
  799.4 2.8 copy.272
  805.4 11.6 %collective-permute-done.98 = bf16[4,64,640]{2,1,0:T(8,128)(2,1)} collective-permute-done((bf16[4,64,640]{2,1,0:T(8,128)(2,1)}, bf16[4,64,640]{2,1,0:T(8,128)(2,1)}, u32[]{:S(2)}, u32[]{:S(2)}) %collective-permute-start.98) | collective-permute-done | bytes 327712 | tf_op jit(solution)/shard_map/ppermute | solution.py:93
  822.1 5.7 collective-permute-start.102
  832.7 2.8 collective-permute-done.101
  (594 shorter events, 294.5 us)
Async XLA Ops:
  7.3 217.7 %all-gather.5.cloned.1.call-start = ((), (), s32[]{:S(2)}) async-start(), calls=%async_computation.11 | async-start | bytes 8650752 | tf_op jit(solution)/shard_map/all_gather | solution.py:786
  8.2 31.7 %collective-permute-start.3 = (bf16[128,2048]{1,0:T(8,128)(2,1)S(1)}, bf16[128,2048]{1,0:T(8,128)(2,1)}, u32[]{:S(2)}, u32[]{:S(2)}) collective-permute-start(bf16[128,2048]{1,0:T(8,128)(2,1)S(1)} %bitcast.323), channel_id=1, source_target_pairs={{0,1},{1,0},{2,3},{3,2},{4,5},{5,4},{6,7},{7,6},{8,9},{9,8},{10,11... | collective-permute-start | bytes 1572872 | tf_op jit(solution)/shard_map/ppermute | solution.py:93
  11.2 28.8 %collective-permute-start.5 = (bf16[128,2048]{1,0:T(8,128)(2,1)S(1)}, bf16[128,2048]{1,0:T(8,128)(2,1)}, u32[]{:S(2)}, u32[]{:S(2)}) collective-permute-start(bf16[128,2048]{1,0:T(8,128)(2,1)S(1)} %bitcast.324), channel_id=1, source_target_pairs={{0,3},{1,2},{2,1},{3,0},{4,7},{5,6},{6,5},{7,4},{8,11},{9,10},{10,... | collective-permute-start | bytes 1572872 | tf_op jit(solution)/shard_map/ppermute | solution.py:93
  12.7 27.3 %collective-permute-start.4 = (bf16[128,2048]{1,0:T(8,128)(2,1)S(1)}, bf16[128,2048]{1,0:T(8,128)(2,1)}, u32[]{:S(2)}, u32[]{:S(2)}) collective-permute-start(bf16[128,2048]{1,0:T(8,128)(2,1)S(1)} %bitcast.325), channel_id=1, source_target_pairs={{0,2},{1,3},{2,0},{3,1},{4,6},{5,7},{6,4},{7,5},{8,10},{9,11},{10,... | collective-permute-start | bytes 1572872 | tf_op jit(solution)/shard_map/ppermute | solution.py:93
  21.9 23.6 %all-to-all-start = ((bf16[8,64,512]{2,1,0:T(8,128)(2,1)}), bf16[8,64,512]{2,1,0:T(8,128)(2,1)}, u32[]{:S(2)}, u32[]{:S(2)}) async-start(bf16[8,64,512]{2,1,0:T(8,128)(2,1)} %maximum_bitcast_fusion), calls=%async_computation | async-start | bytes 1048576 | tf_op jit(solution)/shard_map/all_to_all | solution.py:720
  26.1 198.9 %all-gather.3.cloned.1.call-start = ((), (), s32[]{:S(2)}) async-start(), calls=%async_computation.10 | async-start | bytes 17301504 | tf_op jit(solution)/shard_map/all_gather | solution.py:785
  31.1 77.5 %collective-permute-start.14 = (bf16[64,2048]{1,0:T(8,128)(2,1)}, bf16[64,2048]{1,0:T(8,128)(2,1)}, u32[]{:S(2)}, u32[]{:S(2)}) collective-permute-start(bf16[64,2048]{1,0:T(8,128)(2,1)} %param.25), channel_id=1, source_target_pairs={{0,0},{1,4},{2,8},{3,12},{4,1},{5,5},{6,9},{7,13},{8,2},{9,6},{10,... | collective-permute-start | bytes 786440 | tf_op jit(solution)/shard_map/ppermute | solution.py:704
  53.0 55.9 %all-to-all-start.1 = ((bf16[4,2,256,512]{3,2,1,0:T(8,128)(2,1)}), bf16[4,2,256,512]{3,2,1,0:T(8,128)(2,1)}, u32[]{:S(2)}, u32[]{:S(2)}) async-start(bf16[4,2,256,512]{3,2,1,0:T(8,128)(2,1)} %broadcast_in_dim.172), calls=%async_computation.1 | async-start | bytes 4194304 | tf_op jit(solution)/shard_map/all_to_all | solution.py:133
  61.1 564.2 %reduce-scatter.5.cloned.1.call-start = ((), (), s32[]{:S(2)}) async-start(), calls=%async_computation.12 | async-start | bytes 6291456 | tf_op jit(solution)/shard_map/reduce_scatter | solution.py:973
  83.8 24.9 %collective-permute-start.6 = (bf16[4,128,2048]{2,1,0:T(8,128)(2,1)}, bf16[4,128,2048]{2,1,0:T(8,128)(2,1)}, u32[]{:S(2)}, u32[]{:S(2)}) collective-permute-start(bf16[4,128,2048]{2,1,0:T(8,128)(2,1)} %pad_maximum_fusion.1.near_ref), channel_id=1, source_target_pairs={{0,16},{16,0},{1,17},{17,1},{2,18},{18,2},{3,19},{19,3},{4,20},{20... | collective-permute-start | bytes 6291464 | tf_op jit(solution)/shard_map/ppermute | solution.py:93
  108.9 30.5 %collective-permute-start.16 = (bf16[64,2048]{1,0:T(8,128)(2,1)}, bf16[64,2048]{1,0:T(8,128)(2,1)S(1)}, u32[]{:S(2)}, u32[]{:S(2)}) collective-permute-start(bf16[64,2048]{1,0:T(8,128)(2,1)} %collective-permute-done.14), channel_id=1, source_target_pairs={{0,8},{4,12},{8,0},{12,4},{1,9},{5,13},{9,1},{13,5},{2,10},{6,14},... | collective-permute-start | bytes 786440 | tf_op jit(solution)/shard_map/ppermute | solution.py:93
  110.7 28.7 %collective-permute-start.15 = (bf16[64,2048]{1,0:T(8,128)(2,1)}, bf16[64,2048]{1,0:T(8,128)(2,1)S(1)}, u32[]{:S(2)}, u32[]{:S(2)}) collective-permute-start(bf16[64,2048]{1,0:T(8,128)(2,1)} %collective-permute-done.14), channel_id=1, source_target_pairs={{0,4},{4,0},{8,12},{12,8},{1,5},{5,1},{9,13},{13,9},{2,6},{6,2},{1... | collective-permute-start | bytes 786440 | tf_op jit(solution)/shard_map/ppermute | solution.py:93
  113.2 26.2 %collective-permute-start.17 = (bf16[64,2048]{1,0:T(8,128)(2,1)}, bf16[64,2048]{1,0:T(8,128)(2,1)}, u32[]{:S(2)}, u32[]{:S(2)}) collective-permute-start(bf16[64,2048]{1,0:T(8,128)(2,1)} %collective-permute-done.14), channel_id=1, source_target_pairs={{0,12},{4,8},{8,4},{12,0},{1,13},{5,9},{9,5},{13,1},{2,14},{6,10},... | collective-permute-start | bytes 786440 | tf_op jit(solution)/shard_map/ppermute | solution.py:93
  160.2 25.5 %collective-permute-start.21 = (bf16[128,2048]{1,0:T(8,128)(2,1)}, bf16[128,2048]{1,0:T(8,128)(2,1)}, u32[]{:S(2)}, u32[]{:S(2)}) collective-permute-start(bf16[128,2048]{1,0:T(8,128)(2,1)} %get-tuple-element.615), channel_id=1, source_target_pairs={{0,2},{1,3},{2,0},{3,1},{4,6},{5,7},{6,4},{7,5},{8,10},{9,11},{10,... | collective-permute-start | bytes 1572872 | tf_op jit(solution)/shard_map/ppermute | solution.py:93
  161.0 24.6 %collective-permute-start.22 = (bf16[128,2048]{1,0:T(8,128)(2,1)}, bf16[128,2048]{1,0:T(8,128)(2,1)}, u32[]{:S(2)}, u32[]{:S(2)}) collective-permute-start(bf16[128,2048]{1,0:T(8,128)(2,1)} %get-tuple-element.616), channel_id=1, source_target_pairs={{0,3},{1,2},{2,1},{3,0},{4,7},{5,6},{6,5},{7,4},{8,11},{9,10},{10,... | collective-permute-start | bytes 1572872 | tf_op jit(solution)/shard_map/ppermute | solution.py:93
  190.8 28.3 %collective-permute-start.28 = (bf16[1,128,2048]{2,1,0:T(8,128)(2,1)}, bf16[1,128,2048]{2,1,0:T(8,128)(2,1)}, u32[]{:S(2)}, u32[]{:S(2)}) collective-permute-start(bf16[1,128,2048]{2,1,0:T(8,128)(2,1)} %fusion.58.piece_0), channel_id=1, source_target_pairs={{0,2},{1,3},{2,0},{3,1},{4,6},{5,7},{6,4},{7,5},{8,10},{9,11},{10,... | collective-permute-start | bytes 1572872 | tf_op jit(solution)/shard_map/ppermute | solution.py:93
  192.2 26.9 %collective-permute-start.27 = (bf16[1,128,2048]{2,1,0:T(8,128)(2,1)}, bf16[1,128,2048]{2,1,0:T(8,128)(2,1)}, u32[]{:S(2)}, u32[]{:S(2)}) collective-permute-start(bf16[1,128,2048]{2,1,0:T(8,128)(2,1)} %fusion.58.piece_0), channel_id=1, source_target_pairs={{0,1},{1,0},{2,3},{3,2},{4,5},{5,4},{6,7},{7,6},{8,9},{9,8},{10,11... | collective-permute-start | bytes 1572872 | tf_op jit(solution)/shard_map/ppermute | solution.py:93
  192.8 26.3 %collective-permute-start.29 = (bf16[1,128,2048]{2,1,0:T(8,128)(2,1)}, bf16[1,128,2048]{2,1,0:T(8,128)(2,1)}, u32[]{:S(2)}, u32[]{:S(2)}) collective-permute-start(bf16[1,128,2048]{2,1,0:T(8,128)(2,1)} %fusion.58.piece_0), channel_id=1, source_target_pairs={{0,3},{1,2},{2,1},{3,0},{4,7},{5,6},{6,5},{7,4},{8,11},{9,10},{10,... | collective-permute-start | bytes 1572872 | tf_op jit(solution)/shard_map/ppermute | solution.py:93
  194.4 24.7 %collective-permute-start.26 = (bf16[128,2048]{1,0:T(8,128)(2,1)S(1)}, bf16[128,2048]{1,0:T(8,128)(2,1)}, u32[]{:S(2)}, u32[]{:S(2)}) collective-permute-start(bf16[128,2048]{1,0:T(8,128)(2,1)S(1)} %multiply_convert_fusion), channel_id=1, source_target_pairs={{0,8},{4,12},{8,0},{12,4},{1,9},{5,13},{9,1},{13,5},{2,10},{6,14},... | collective-permute-start | bytes 1572872 | tf_op jit(solution)/shard_map/ppermute | solution.py:93
  219.1 24.1 %collective-permute-start.33 = (bf16[1,128,2048]{2,1,0:T(8,128)(2,1)}, bf16[1,128,2048]{2,1,0:T(8,128)(2,1)S(1)}, u32[]{:S(2)}, u32[]{:S(2)}) collective-permute-start(bf16[1,128,2048]{2,1,0:T(8,128)(2,1)} %bitcast.62.piece_0), channel_id=1, source_target_pairs={{0,2},{1,3},{2,0},{3,1},{4,6},{5,7},{6,4},{7,5},{8,10},{9,11},{10,... | collective-permute-start | bytes 1572872 | tf_op jit(solution)/shard_map/ppermute | solution.py:93
  221.1 24.6 %collective-permute-start.34 = (bf16[1,128,2048]{2,1,0:T(8,128)(2,1)}, bf16[1,128,2048]{2,1,0:T(8,128)(2,1)}, u32[]{:S(2)}, u32[]{:S(2)}) collective-permute-start(bf16[1,128,2048]{2,1,0:T(8,128)(2,1)} %bitcast.62.piece_0), channel_id=1, source_target_pairs={{0,3},{1,2},{2,1},{3,0},{4,7},{5,6},{6,5},{7,4},{8,11},{9,10},{10,... | collective-permute-start | bytes 1572872 | tf_op jit(solution)/shard_map/ppermute | solution.py:93
  247.2 25.3 %collective-permute-start.37 = (bf16[2,128,2048]{2,1,0:T(8,128)(2,1)S(1)}, bf16[2,128,2048]{2,1,0:T(8,128)(2,1)S(1)}, u32[]{:S(2)}, u32[]{:S(2)}) collective-permute-start(bf16[2,128,2048]{2,1,0:T(8,128)(2,1)S(1)} %get-tuple-element.669), channel_id=1, source_target_pairs={{0,2},{1,3},{2,0},{3,1},{4,6},{5,7},{6,4},{7,5},{8,10},{9,11},{10,... | collective-permute-start | bytes 3145736 | tf_op jit(solution)/shard_map/ppermute | solution.py:93
  248.9 26.1 %collective-permute-start.36 = (bf16[2,128,2048]{2,1,0:T(8,128)(2,1)S(1)}, bf16[2,128,2048]{2,1,0:T(8,128)(2,1)S(1)}, u32[]{:S(2)}, u32[]{:S(2)}) collective-permute-start(bf16[2,128,2048]{2,1,0:T(8,128)(2,1)S(1)} %get-tuple-element.670), channel_id=1, source_target_pairs={{0,1},{1,0},{2,3},{3,2},{4,5},{5,4},{6,7},{7,6},{8,9},{9,8},{10,11... | collective-permute-start | bytes 3145736 | tf_op jit(solution)/shard_map/ppermute | solution.py:93
  249.2 37.0 %collective-permute-start.40 = (bf16[1,128,2048]{2,1,0:T(8,128)(2,1)}, bf16[1,128,2048]{2,1,0:T(8,128)(2,1)}, u32[]{:S(2)}, u32[]{:S(2)}) collective-permute-start(bf16[1,128,2048]{2,1,0:T(8,128)(2,1)} %get-tuple-element.299), channel_id=1, source_target_pairs={{0,3},{1,2},{2,1},{3,0},{4,7},{5,6},{6,5},{7,4},{8,11},{9,10},{10,... | collective-permute-start | bytes 1572872 | tf_op jit(solution)/shard_map/ppermute | solution.py:93
  250.7 39.5 %collective-permute-start.35 = (bf16[128,2048]{1,0:T(8,128)(2,1)S(1)}, bf16[128,2048]{1,0:T(8,128)(2,1)S(1)}, u32[]{:S(2)}, u32[]{:S(2)}) collective-permute-start(bf16[128,2048]{1,0:T(8,128)(2,1)S(1)} %multiply_convert_fusion), channel_id=1, source_target_pairs={{0,4},{4,0},{8,12},{12,8},{1,5},{5,1},{9,13},{13,9},{2,6},{6,2},{1... | collective-permute-start | bytes 1572872 | tf_op jit(solution)/shard_map/ppermute | solution.py:93
  291.5 32.4 %collective-permute-start.42 = (bf16[2,128,2048]{2,1,0:T(8,128)(2,1)}, bf16[2,128,2048]{2,1,0:T(8,128)(2,1)S(1)}, u32[]{:S(2)}, u32[]{:S(2)}) collective-permute-start(bf16[2,128,2048]{2,1,0:T(8,128)(2,1)} %get-tuple-element.667), channel_id=1, source_target_pairs={{0,2},{1,3},{2,0},{3,1},{4,6},{5,7},{6,4},{7,5},{8,10},{9,11},{10,... | collective-permute-start | bytes 3145736 | tf_op jit(solution)/shard_map/ppermute | solution.py:93
  292.9 30.9 %collective-permute-start.41 = (bf16[2,128,2048]{2,1,0:T(8,128)(2,1)S(1)}, bf16[2,128,2048]{2,1,0:T(8,128)(2,1)S(1)}, u32[]{:S(2)}, u32[]{:S(2)}) collective-permute-start(bf16[2,128,2048]{2,1,0:T(8,128)(2,1)S(1)} %get-tuple-element.668), channel_id=1, source_target_pairs={{0,1},{1,0},{2,3},{3,2},{4,5},{5,4},{6,7},{7,6},{8,9},{9,8},{10,11... | collective-permute-start | bytes 3145736 | tf_op jit(solution)/shard_map/ppermute | solution.py:93
  293.2 36.4 %collective-permute-start.45 = (bf16[1,128,2048]{2,1,0:T(8,128)(2,1)}, bf16[1,128,2048]{2,1,0:T(8,128)(2,1)S(1)}, u32[]{:S(2)}, u32[]{:S(2)}) collective-permute-start(bf16[1,128,2048]{2,1,0:T(8,128)(2,1)} %get-tuple-element.314), channel_id=1, source_target_pairs={{0,3},{1,2},{2,1},{3,0},{4,7},{5,6},{6,5},{7,4},{8,11},{9,10},{10,... | collective-permute-start | bytes 1572872 | tf_op jit(solution)/shard_map/ppermute | solution.py:93
  333.0 23.2 %collective-permute-start.46 = (bf16[1,128,2048]{2,1,0:T(8,128)(2,1)}, bf16[1,128,2048]{2,1,0:T(8,128)(2,1)S(1)}, u32[]{:S(2)}, u32[]{:S(2)}) collective-permute-start(bf16[1,128,2048]{2,1,0:T(8,128)(2,1)} %get-tuple-element.326), channel_id=1, source_target_pairs={{0,1},{1,0},{2,3},{3,2},{4,5},{5,4},{6,7},{7,6},{8,9},{9,8},{10,11... | collective-permute-start | bytes 1572872 | tf_op jit(solution)/shard_map/ppermute | solution.py:93
  358.8 24.8 %collective-permute-start.51 = (bf16[1,128,2048]{2,1,0:T(8,128)(2,1)S(1)}, bf16[1,128,2048]{2,1,0:T(8,128)(2,1)S(1)}, u32[]{:S(2)}, u32[]{:S(2)}) collective-permute-start(bf16[1,128,2048]{2,1,0:T(8,128)(2,1)S(1)} %copy-done.88), channel_id=1, source_target_pairs={{0,2},{1,3},{2,0},{3,1},{4,6},{5,7},{6,4},{7,5},{8,10},{9,11},{10,... | collective-permute-start | bytes 1572872 | tf_op jit(solution)/shard_map/ppermute | solution.py:93
  359.9 23.6 %collective-permute-start.52 = (bf16[1,128,2048]{2,1,0:T(8,128)(2,1)S(1)}, bf16[1,128,2048]{2,1,0:T(8,128)(2,1)S(1)}, u32[]{:S(2)}, u32[]{:S(2)}) collective-permute-start(bf16[1,128,2048]{2,1,0:T(8,128)(2,1)S(1)} %copy-done.87), channel_id=1, source_target_pairs={{0,3},{1,2},{2,1},{3,0},{4,7},{5,6},{6,5},{7,4},{8,11},{9,10},{10,... | collective-permute-start | bytes 1572872 | tf_op jit(solution)/shard_map/ppermute | solution.py:93
  361.3 22.6 %collective-permute-start.53 = (bf16[128,2048]{1,0:T(8,128)(2,1)S(1)}, bf16[128,2048]{1,0:T(8,128)(2,1)S(1)}, u32[]{:S(2)}, u32[]{:S(2)}) collective-permute-start(bf16[128,2048]{1,0:T(8,128)(2,1)S(1)} %bitcast.393), channel_id=1, source_target_pairs={{0,12},{4,8},{8,4},{12,0},{1,13},{5,9},{9,5},{13,1},{2,14},{6,10},... | collective-permute-start | bytes 1572872 | tf_op jit(solution)/shard_map/ppermute | solution.py:93
  402.3 23.8 %collective-permute-start.55 = (bf16[128,2048]{1,0:T(8,128)(2,1)}, bf16[128,2048]{1,0:T(8,128)(2,1)S(1)}, u32[]{:S(2)}, u32[]{:S(2)}) collective-permute-start(bf16[128,2048]{1,0:T(8,128)(2,1)} %fusion.24), channel_id=1, source_target_pairs={{0,8},{4,12},{8,0},{12,4},{1,9},{5,13},{9,1},{13,5},{2,10},{6,14},... | collective-permute-start | bytes 1572872 | tf_op jit(solution)/shard_map/ppermute | solution.py:93
  428.5 23.9 %collective-permute-start.62 = (bf16[1,128,2048]{2,1,0:T(8,128)(2,1)S(1)}, bf16[1,128,2048]{2,1,0:T(8,128)(2,1)S(1)}, u32[]{:S(2)}, u32[]{:S(2)}) collective-permute-start(bf16[1,128,2048]{2,1,0:T(8,128)(2,1)S(1)} %bitcast.377), channel_id=1, source_target_pairs={{0,3},{1,2},{2,1},{3,0},{4,7},{5,6},{6,5},{7,4},{8,11},{9,10},{10,... | collective-permute-start | bytes 1572872 | tf_op jit(solution)/shard_map/ppermute | solution.py:93
  455.2 25.9 %collective-permute-start.65 = (bf16[2,128,2048]{2,1,0:T(8,128)(2,1)}, bf16[2,128,2048]{2,1,0:T(8,128)(2,1)S(1)}, u32[]{:S(2)}, u32[]{:S(2)}) collective-permute-start(bf16[2,128,2048]{2,1,0:T(8,128)(2,1)} %get-tuple-element.665), channel_id=1, source_target_pairs={{0,2},{1,3},{2,0},{3,1},{4,6},{5,7},{6,4},{7,5},{8,10},{9,11},{10,... | collective-permute-start | bytes 3145736 | tf_op jit(solution)/shard_map/ppermute | solution.py:93
  455.8 26.3 %collective-permute-start.64 = (bf16[2,128,2048]{2,1,0:T(8,128)(2,1)}, bf16[2,128,2048]{2,1,0:T(8,128)(2,1)S(1)}, u32[]{:S(2)}, u32[]{:S(2)}) collective-permute-start(bf16[2,128,2048]{2,1,0:T(8,128)(2,1)} %get-tuple-element.666), channel_id=1, source_target_pairs={{0,1},{1,0},{2,3},{3,2},{4,5},{5,4},{6,7},{7,6},{8,9},{9,8},{10,11... | collective-permute-start | bytes 3145736 | tf_op jit(solution)/shard_map/ppermute | solution.py:93
  457.6 36.7 %collective-permute-start.68 = (bf16[1,128,2048]{2,1,0:T(8,128)(2,1)}, bf16[1,128,2048]{2,1,0:T(8,128)(2,1)S(1)}, u32[]{:S(2)}, u32[]{:S(2)}) collective-permute-start(bf16[1,128,2048]{2,1,0:T(8,128)(2,1)} %get-tuple-element.372), channel_id=1, source_target_pairs={{0,3},{1,2},{2,1},{3,0},{4,7},{5,6},{6,5},{7,4},{8,11},{9,10},{10,... | collective-permute-start | bytes 1572872 | tf_op jit(solution)/shard_map/ppermute | solution.py:93
  458.8 39.3 %collective-permute-start.63 = (bf16[128,2048]{1,0:T(8,128)(2,1)}, bf16[128,2048]{1,0:T(8,128)(2,1)S(1)}, u32[]{:S(2)}, u32[]{:S(2)}) collective-permute-start(bf16[128,2048]{1,0:T(8,128)(2,1)} %fusion.24), channel_id=1, source_target_pairs={{0,4},{4,0},{8,12},{12,8},{1,5},{5,1},{9,13},{13,9},{2,6},{6,2},{1... | collective-permute-start | bytes 1572872 | tf_op jit(solution)/shard_map/ppermute | solution.py:93
  499.4 32.4 %collective-permute-start.70 = (bf16[2,128,2048]{2,1,0:T(8,128)(2,1)}, bf16[2,128,2048]{2,1,0:T(8,128)(2,1)S(1)}, u32[]{:S(2)}, u32[]{:S(2)}) collective-permute-start(bf16[2,128,2048]{2,1,0:T(8,128)(2,1)} %get-tuple-element.663), channel_id=1, source_target_pairs={{0,2},{1,3},{2,0},{3,1},{4,6},{5,7},{6,4},{7,5},{8,10},{9,11},{10,... | collective-permute-start | bytes 3145736 | tf_op jit(solution)/shard_map/ppermute | solution.py:93
  500.1 31.6 %collective-permute-start.69 = (bf16[2,128,2048]{2,1,0:T(8,128)(2,1)S(1)}, bf16[2,128,2048]{2,1,0:T(8,128)(2,1)S(1)}, u32[]{:S(2)}, u32[]{:S(2)}) collective-permute-start(bf16[2,128,2048]{2,1,0:T(8,128)(2,1)S(1)} %get-tuple-element.664), channel_id=1, source_target_pairs={{0,1},{1,0},{2,3},{3,2},{4,5},{5,4},{6,7},{7,6},{8,9},{9,8},{10,11... | collective-permute-start | bytes 3145736 | tf_op jit(solution)/shard_map/ppermute | solution.py:93
  502.2 35.3 %collective-permute-start.73 = (bf16[1,128,2048]{2,1,0:T(8,128)(2,1)}, bf16[1,128,2048]{2,1,0:T(8,128)(2,1)S(1)}, u32[]{:S(2)}, u32[]{:S(2)}) collective-permute-start(bf16[1,128,2048]{2,1,0:T(8,128)(2,1)} %get-tuple-element.391), channel_id=1, source_target_pairs={{0,3},{1,2},{2,1},{3,0},{4,7},{5,6},{6,5},{7,4},{8,11},{9,10},{10,... | collective-permute-start | bytes 1572872 | tf_op jit(solution)/shard_map/ppermute | solution.py:93
  540.5 24.6 %collective-permute-start.74 = (bf16[1,128,2048]{2,1,0:T(8,128)(2,1)}, bf16[1,128,2048]{2,1,0:T(8,128)(2,1)S(1)}, u32[]{:S(2)}, u32[]{:S(2)}) collective-permute-start(bf16[1,128,2048]{2,1,0:T(8,128)(2,1)} %get-tuple-element.405), channel_id=1, source_target_pairs={{0,1},{1,0},{2,3},{3,2},{4,5},{5,4},{6,7},{7,6},{8,9},{9,8},{10,11... | collective-permute-start | bytes 1572872 | tf_op jit(solution)/shard_map/ppermute | solution.py:93
  542.2 22.9 %collective-permute-start.75 = (bf16[1,128,2048]{2,1,0:T(8,128)(2,1)}, bf16[1,128,2048]{2,1,0:T(8,128)(2,1)S(1)}, u32[]{:S(2)}, u32[]{:S(2)}) collective-permute-start(bf16[1,128,2048]{2,1,0:T(8,128)(2,1)} %get-tuple-element.406), channel_id=1, source_target_pairs={{0,2},{1,3},{2,0},{3,1},{4,6},{5,7},{6,4},{7,5},{8,10},{9,11},{10,... | collective-permute-start | bytes 1572872 | tf_op jit(solution)/shard_map/ppermute | solution.py:93
  566.2 23.2 %collective-permute-start.78 = (bf16[1,128,2048]{2,1,0:T(8,128)(2,1)}, bf16[1,128,2048]{2,1,0:T(8,128)(2,1)}, u32[]{:S(2)}, u32[]{:S(2)}) collective-permute-start(bf16[1,128,2048]{2,1,0:T(8,128)(2,1)} %get-tuple-element.410), channel_id=1, source_target_pairs={{0,1},{1,0},{2,3},{3,2},{4,5},{5,4},{6,7},{7,6},{8,9},{9,8},{10,11... | collective-permute-start | bytes 1572872 | tf_op jit(solution)/shard_map/ppermute | solution.py:93
  568.2 23.1 %collective-permute-start.79 = (bf16[1,128,2048]{2,1,0:T(8,128)(2,1)}, bf16[1,128,2048]{2,1,0:T(8,128)(2,1)}, u32[]{:S(2)}, u32[]{:S(2)}) collective-permute-start(bf16[1,128,2048]{2,1,0:T(8,128)(2,1)} %get-tuple-element.411), channel_id=1, source_target_pairs={{0,2},{1,3},{2,0},{3,1},{4,6},{5,7},{6,4},{7,5},{8,10},{9,11},{10,... | collective-permute-start | bytes 1572872 | tf_op jit(solution)/shard_map/ppermute | solution.py:93
  568.8 22.5 %collective-permute-start.80 = (bf16[1,128,2048]{2,1,0:T(8,128)(2,1)}, bf16[1,128,2048]{2,1,0:T(8,128)(2,1)}, u32[]{:S(2)}, u32[]{:S(2)}) collective-permute-start(bf16[1,128,2048]{2,1,0:T(8,128)(2,1)} %get-tuple-element.412), channel_id=1, source_target_pairs={{0,3},{1,2},{2,1},{3,0},{4,7},{5,6},{6,5},{7,4},{8,11},{9,10},{10,... | collective-permute-start | bytes 1572872 | tf_op jit(solution)/shard_map/ppermute | solution.py:93
  569.8 24.3 %collective-permute-start.81 = (bf16[128,2048]{1,0:T(8,128)(2,1)}, bf16[128,2048]{1,0:T(8,128)(2,1)}, u32[]{:S(2)}, u32[]{:S(2)}) collective-permute-start(bf16[128,2048]{1,0:T(8,128)(2,1)} %bitcast.283), channel_id=1, source_target_pairs={{0,12},{4,8},{8,4},{12,0},{1,13},{5,9},{9,5},{13,1},{2,14},{6,10},... | collective-permute-start | bytes 1572872 | tf_op jit(solution)/shard_map/ppermute | solution.py:93
  594.1 178.9 %reduce-scatter.7.cloned.1.call-start = ((), (), s32[]{:S(2)}) async-start(), calls=%async_computation.13 | async-start | bytes 3145728 | tf_op jit(solution)/shard_map/reduce_scatter | solution.py:970
  598.8 239.0 %reduce-scatter.11.cloned.1.call-start = ((), (), s32[]{:S(2)}) async-start(), calls=%async_computation.15 | async-start | bytes 17301504 | tf_op jit(solution)/shard_map/reduce_scatter | solution.py:967
  621.8 37.3 %collective-permute-start.85 = (bf16[128,2048]{1,0:T(8,128)(2,1)}, bf16[128,2048]{1,0:T(8,128)(2,1)S(1)}, u32[]{:S(2)}, u32[]{:S(2)}) collective-permute-start(bf16[128,2048]{1,0:T(8,128)(2,1)} %get-tuple-element.605), channel_id=1, source_target_pairs={{0,2},{1,3},{2,0},{3,1},{4,6},{5,7},{6,4},{7,5},{8,10},{9,11},{10,... | collective-permute-start | bytes 1572872 | tf_op jit(solution)/shard_map/ppermute | solution.py:93
  623.3 35.8 %collective-permute-start.84 = (bf16[128,2048]{1,0:T(8,128)(2,1)}, bf16[128,2048]{1,0:T(8,128)(2,1)S(1)}, u32[]{:S(2)}, u32[]{:S(2)}) collective-permute-start(bf16[128,2048]{1,0:T(8,128)(2,1)} %get-tuple-element.605), channel_id=1, source_target_pairs={{0,1},{1,0},{2,3},{3,2},{4,5},{5,4},{6,7},{7,6},{8,9},{9,8},{10,11... | collective-permute-start | bytes 1572872 | tf_op jit(solution)/shard_map/ppermute | solution.py:93
  624.7 34.3 %collective-permute-start.86 = (bf16[128,2048]{1,0:T(8,128)(2,1)}, bf16[128,2048]{1,0:T(8,128)(2,1)S(1)}, u32[]{:S(2)}, u32[]{:S(2)}) collective-permute-start(bf16[128,2048]{1,0:T(8,128)(2,1)} %get-tuple-element.605), channel_id=1, source_target_pairs={{0,3},{1,2},{2,1},{3,0},{4,7},{5,6},{6,5},{7,4},{8,11},{9,10},{10,... | collective-permute-start | bytes 1572872 | tf_op jit(solution)/shard_map/ppermute | solution.py:93
  628.5 33.4 %all-to-all-start.3 = ((bf16[16,64,352]{2,1,0:T(8,128)(2,1)}), bf16[16,64,352]{2,1,0:T(8,128)(2,1)S(1)}, u32[]{:S(2)}, u32[]{:S(2)}) async-start(bf16[16,64,352]{2,1,0:T(8,128)(2,1)} %bitcast.133), calls=%async_computation.4 | async-start | bytes 1572864 | tf_op jit(solution)/shard_map/all_to_all | solution.py:983
  634.6 203.1 %reduce-scatter.9.cloned.1.call-start = ((), (), s32[]{:S(2)}) async-start(), calls=%async_computation.14 | async-start | bytes 34603008 | tf_op jit(solution)/shard_map/reduce_scatter | solution.py:1006
  677.0 25.1 %collective-permute-start.88 = (bf16[64,2048]{1,0:T(8,128)(2,1)S(1)}, bf16[64,2048]{1,0:T(8,128)(2,1)S(1)}, u32[]{:S(2)}, u32[]{:S(2)}) collective-permute-start(bf16[64,2048]{1,0:T(8,128)(2,1)S(1)} %get-tuple-element.628), channel_id=1, source_target_pairs={{0,4},{4,0},{8,12},{12,8},{1,5},{5,1},{9,13},{13,9},{2,6},{6,2},{1... | collective-permute-start | bytes 786440 | tf_op jit(solution)/shard_map/ppermute | solution.py:93
  678.9 23.2 %collective-permute-start.90 = (bf16[64,2048]{1,0:T(8,128)(2,1)S(1)}, bf16[64,2048]{1,0:T(8,128)(2,1)S(1)}, u32[]{:S(2)}, u32[]{:S(2)}) collective-permute-start(bf16[64,2048]{1,0:T(8,128)(2,1)S(1)} %get-tuple-element.629), channel_id=1, source_target_pairs={{0,12},{4,8},{8,4},{12,0},{1,13},{5,9},{9,5},{13,1},{2,14},{6,10},... | collective-permute-start | bytes 786440 | tf_op jit(solution)/shard_map/ppermute | solution.py:93
  681.3 23.3 %collective-permute-start.89 = (bf16[64,2048]{1,0:T(8,128)(2,1)S(1)}, bf16[64,2048]{1,0:T(8,128)(2,1)S(1)}, u32[]{:S(2)}, u32[]{:S(2)}) collective-permute-start(bf16[64,2048]{1,0:T(8,128)(2,1)S(1)} %get-tuple-element.630), channel_id=1, source_target_pairs={{0,8},{4,12},{8,0},{12,4},{1,9},{5,13},{9,1},{13,5},{2,10},{6,14},... | collective-permute-start | bytes 786440 | tf_op jit(solution)/shard_map/ppermute | solution.py:93
  716.2 32.3 %collective-permute-start.93 = (bf16[128,2688]{1,0:T(8,128)(2,1)}, bf16[128,2688]{1,0:T(8,128)(2,1)}, u32[]{:S(2)}, u32[]{:S(2)}) collective-permute-start(bf16[128,2688]{1,0:T(8,128)(2,1)} %get-tuple-element.610), channel_id=1, source_target_pairs={{0,2},{1,3},{2,0},{3,1},{4,6},{5,7},{6,4},{7,5},{8,10},{9,11},{10,... | collective-permute-start | bytes 2064392 | tf_op jit(solution)/shard_map/ppermute | solution.py:93
  717.7 30.8 %collective-permute-start.94 = (bf16[128,2688]{1,0:T(8,128)(2,1)}, bf16[128,2688]{1,0:T(8,128)(2,1)}, u32[]{:S(2)}, u32[]{:S(2)}) collective-permute-start(bf16[128,2688]{1,0:T(8,128)(2,1)} %get-tuple-element.611), channel_id=1, source_target_pairs={{0,3},{1,2},{2,1},{3,0},{4,7},{5,6},{6,5},{7,4},{8,11},{9,10},{10,... | collective-permute-start | bytes 2064392 | tf_op jit(solution)/shard_map/ppermute | solution.py:93
  723.6 54.1 %all-to-all-start.4 = ((bf16[4,2,256,512]{3,2,1,0:T(8,128)(2,1)}), bf16[4,2,256,512]{3,2,1,0:T(8,128)(2,1)}, u32[]{:S(2)}, u32[]{:S(2)}) async-start(bf16[4,2,256,512]{3,2,1,0:T(8,128)(2,1)} %copy_bitcast_fusion), calls=%async_computation.5 | async-start | bytes 4194304 | tf_op jit(solution)/shard_map/all_to_all | solution.py:1034
  780.6 37.7 %all-to-all-start.5 = ((bf16[8,64,512]{2,1,0:T(8,128)(2,1)}), bf16[8,64,512]{2,1,0:T(8,128)(2,1)}, u32[]{:S(2)}, u32[]{:S(2)}) async-start(bf16[8,64,512]{2,1,0:T(8,128)(2,1)} %bitcast.345), calls=%async_computation.6 | async-start | bytes 1048576 | tf_op jit(solution)/shard_map/all_to_all | solution.py:1083
  787.8 29.2 %collective-permute-start.98 = (bf16[4,64,640]{2,1,0:T(8,128)(2,1)}, bf16[4,64,640]{2,1,0:T(8,128)(2,1)}, u32[]{:S(2)}, u32[]{:S(2)}) collective-permute-start(bf16[4,64,640]{2,1,0:T(8,128)(2,1)} %get-tuple-element.624), channel_id=1, source_target_pairs={{0,3},{1,2},{2,1},{3,0},{4,7},{5,6},{6,5},{7,4},{8,11},{9,10},{10,... | collective-permute-start | bytes 983048 | tf_op jit(solution)/shard_map/ppermute | solution.py:93
  789.3 27.7 %collective-permute-start.97 = (bf16[4,64,640]{2,1,0:T(8,128)(2,1)}, bf16[4,64,640]{2,1,0:T(8,128)(2,1)}, u32[]{:S(2)}, u32[]{:S(2)}) collective-permute-start(bf16[4,64,640]{2,1,0:T(8,128)(2,1)} %get-tuple-element.625), channel_id=1, source_target_pairs={{0,2},{1,3},{2,0},{3,1},{4,6},{5,7},{6,4},{7,5},{8,10},{9,11},{10,... | collective-permute-start | bytes 983048 | tf_op jit(solution)/shard_map/ppermute | solution.py:93
  792.2 26.1 %collective-permute-start.99 = (bf16[64,2048]{1,0:T(8,128)(2,1)}, bf16[64,2048]{1,0:T(8,128)(2,1)}, u32[]{:S(2)}, u32[]{:S(2)}) collective-permute-start(bf16[64,2048]{1,0:T(8,128)(2,1)} %fusion.22), channel_id=1, source_target_pairs={{0,0},{4,1},{8,2},{12,3},{1,4},{5,5},{9,6},{13,7},{2,8},{6,9},{10,... | collective-permute-start | bytes 786440 | tf_op jit(solution)/shard_map/ppermute | solution.py:1091
  (143 other events, 1602.5 us)
Sparse Core Ops, SparseCore 0:
  9.7 18.7 all-gather.4
  30.0 25.0 all-gather.2
  594.2 9.9 reduce-scatter.4
  606.3 10.8 reduce-scatter.6
  620.0 21.3 reduce-scatter.10
  662.1 34.3 reduce-scatter.8
where the time goes:
time: 855 us; the launch traced here: 846 us
  Pallas kernels  243 us (28%)
  waiting for transfers between devices  222 us (26%)
  starting transfers between devices  156 us (18%)
  local copies, waits for them, and re-layouts  105 us (12%)
  other arithmetic  83.7 us (10%)
  between operations  20.4 us (2%)
  matrix products  16.2 us (2%)
    ppermute x101, waiting for transfers between devices, hop(): return straight(lax.ppermute(straight(values), axis, moves))  218 us
    ppermute x101, starting transfers between devices, hop(): return straight(lax.ppermute(straight(values), axis, moves))  118 us
    pallas_call x4, Pallas kernels, expert_forward(): pl.pallas_call(body, in_specs=[pl.BlockSpec(memory_space=pltpu.VMEM)] * 3...  73.3 us
    pallas_call x4, Pallas kernels, expert_backward(): pl.pallas_call(body, in_specs=[pl.BlockSpec(memory_space=pltpu.VMEM)] * 2...  72.5 us
    pallas_call x5, Pallas kernels, sums_of_products(): pl.pallas_call(body, grid=(width // wide, height // tall), in_specs=[pl.B...  60.1 us
    pallas_call x1, Pallas kernels, attend_back(): pl.pallas_call(body, grid=(sequences,), in_specs=[halves(width), halves(w...  20.7 us
  transfers between devices with their start and end apart: 115, of which 44 were waited for; matrix products, arithmetic and copies ran while one was open for 22% of the time, Pallas kernels for 29%

commit v1 on v0

--- a/solution.py
+++ b/solution.py
@@ -476,7 +476,7 @@
     def body(
         near_ref, away_ref, gain_ref, down_ref, latent_gain_ref, query_ref, up_ref, cos_ref, sin_ref, place_ref, places_ref, early_ref,
         normed_ref, latent_ref, compressed_ref, queries_ref, rope_ref, keyval_ref,
-        attention_ref, context_ref,
+        attention_ref, near_context_ref, away_context_ref,
     ):
         for side, ref in enumerate((near_ref, away_ref)):
             values = ref[0].astype(F32)
@@ -504,9 +504,11 @@
             weights = jnp.exp(scores - jnp.max(scores, axis=1, keepdims=True))
             attention = weights / jnp.sum(weights, axis=1, keepdims=True)
             attention_ref[0, head] = attention
-            context_ref[:, head * DV : (head + 1) * DV] = dot_plain(
+            context = dot_plain(
                 attention.astype(BF), keyval_ref[:, start + DN : start + DN + DV]
             ).astype(BF)
+            near_context_ref[0, :, head * DV : (head + 1) * DV] = context[:rows]
+            away_context_ref[0, :, head * DV : (head + 1) * DV] = context[rows:]
 
     def by_rows(columns):
         return pl.BlockSpec((length, columns), lambda s: (s, 0))
@@ -527,12 +529,14 @@
         out_specs=[by_rows(c) for c in columns]
         + [
             pl.BlockSpec((1, heads, length, length), lambda s: (s, 0, 0, 0)),
-            by_rows(heads * DV),
+            pl.BlockSpec((1, rows, heads * DV), lambda s: (s, 0, 0)),
+            pl.BlockSpec((1, rows, heads * DV), lambda s: (s, 0, 0)),
         ],
         out_shape=[jax.ShapeDtypeStruct((every, c), k) for c, k in zip(columns, kinds)]
         + [
             jax.ShapeDtypeStruct((sequences, heads, length, length), F32),
-            jax.ShapeDtypeStruct((every, heads * DV), BF),
+            jax.ShapeDtypeStruct((sequences, rows, heads * DV), BF),
+            jax.ShapeDtypeStruct((sequences, rows, heads * DV), BF),
         ],
         compiler_params=pltpu.CompilerParams(vmem_limit_bytes=ROOM),
         cost_estimate=pl.CostEstimate(
@@ -776,7 +780,7 @@
     up_weight = packed[:, wide_q:].reshape(KVR, fold * up_fold)
 
 
-    normed, latent, compressed, queries, key_rope, keyval, attention, context = attend(
+    normed, latent, compressed, queries, key_rope, keyval, attention, *context = attend(
         near_rows, away_rows, gain_one_f[None], small, latent_gain_f[None], query_weight,
         up_weight, heads, spread_cos, spread_sin,
         jnp.broadcast_to(places[:, None], (seq_length, 128)),
@@ -808,10 +812,10 @@
     context, output_weight, chunk_select, chunk_masks = stage(
         context, output_weight, chunk_select, chunk_masks
     )
-    sides = context.reshape(PLANE, cores, token_rows, heads * DV)
+    sides = [side.reshape(PLANE * token_rows, heads * DV) for side in context]
 
     def project(side):
-        flat = sides[:, side].reshape(PLANE * token_rows, heads * DV)
+        flat = sides[side]
         return dot_plain(flat, output_weight).reshape(PLANE, token_rows, model_width)
 
     given_part = hop(project(1).astype(BF), "fsdp", 1)
@@ -1009,7 +1013,7 @@
     away_grad = hop(near_grad, "fsdp", 1)
     flat = (PLANE * token_rows, model_width)
     grad_output_weight = sums_of_products(
-        [sides[:, 0].reshape(flat[0], -1), sides[:, 1].reshape(flat[0], -1)],
+        sides,
         [near_grad.reshape(flat), away_grad.reshape(flat)],
         heads * DV,
         512,

time: 855 us -> 854 us (level)
  transfers between devices with their start and end apart: 115 -> 115, of which waited for: 44 -> 44; matrix products, arithmetic and copies ran while one was open for 22% -> 21% of each run, Pallas kernels for 29% -> 29%
where the time goes in v1:
time: 854 us; the launch traced here: 846 us
  Pallas kernels  243 us (28%)
  waiting for transfers between devices  224 us (26%)
  starting transfers between devices  156 us (18%)
  local copies, waits for them, and re-layouts  102 us (12%)
  other arithmetic  83.6 us (10%)
  between operations  20.4 us (2%)
  matrix products  16.2 us (2%)
    ppermute x101, waiting for transfers between devices, hop(): return straight(lax.ppermute(straight(values), axis, moves))  220 us
    ppermute x101, starting transfers between devices, hop(): return straight(lax.ppermute(straight(values), axis, moves))  117 us
    pallas_call x4, Pallas kernels, expert_forward(): pl.pallas_call(body, in_specs=[pl.BlockSpec(memory_space=pltpu.VMEM)] * 3...  73.2 us
    pallas_call x4, Pallas kernels, expert_backward(): pl.pallas_call(body, in_specs=[pl.BlockSpec(memory_space=pltpu.VMEM)] * 2...  72.4 us
    pallas_call x5, Pallas kernels, sums_of_products(): pl.pallas_call(body, grid=(width // wide, height // tall), in_specs=[pl.B...  60.3 us
    pallas_call x1, Pallas kernels, attend_back(): pl.pallas_call(body, grid=(sequences,), in_specs=[halves(width), halves(w...  20.7 us
  transfers between devices with their start and end apart: 115, of which 44 were waited for; matrix products, arithmetic and copies ran while one was open for 21% of the time, Pallas kernels for 29%

profile of v1, /device:TPU:0, one launch (start us, length us, event | category | flops | bytes accessed | tf_op | source)
XLA Modules:
  0.0 845.7 jit_solution(18389238540009824025)
XLA Ops:
  8.2 2.9 collective-permute-start.3
  21.9 4.2 all-to-all-start
  31.1 3.6 collective-permute-start.14
  34.7 4.2 collective-permute-done.1
  40.0 3.4 pad_maximum_fusion.1.near_ref
  45.5 4.8 collective-permute-start.7
  53.0 8.1 all-to-all-start.1
  61.6 6.9 collective-permute-done.9
  92.7 3.4 collective-permute-start.13
  122.6 16.4 %shard_map.298 = (bf16[1024,2048]{1,0:T(8,128)(2,1)}, f32[1024,640]{1,0:T(8,128)}, bf16[1024,512]{1,0:T(8,128)(2,1)}, bf16[1024,384]{1,0:T(8,128)(2,1)}, bf16[10...) custom-call(bf16[4,128,2048]{2,1,0:T(8,128)(2,1)} %pad_maximum_fusio, ...), custom_call_target="tpu_custom_call" | custom-call | flops 4831838208 | bytes 33554432 | tf_op jit(solution)/shard_map/pallas_call | solution.py:523
  144.8 3.4 collective-permute-done.19
  152.3 3.7 collective-permute-start.25
  166.6 6.3 collective-permute-done.24
  176.1 8.9 %collective-permute-done.21 = bf16[128,2048]{1,0:T(8,128)(2,1)} collective-permute-done((bf16[128,2048]{1,0:T(8,128)(2,1)}, bf16[128,2048]{1,0:T(8,128)(2,1)}, u32[]{:S(2)}, u32[]{:S(2)}) %collective-permute-start.21) | collective-permute-done | bytes 524320 | tf_op jit(solution)/shard_map/ppermute | solution.py:93
  197.5 21.0 %collective-permute-done.26 = bf16[128,2048]{1,0:T(8,128)(2,1)} collective-permute-done((bf16[128,2048]{1,0:T(8,128)(2,1)S(1)}, bf16[128,2048]{1,0:T(8,128)(2,1)}, u32[]{:S(2)}, u32[]{:S(2)}) %collective-permute-start.26) | collective-permute-done | bytes 524320 | tf_op jit(solution)/shard_map/ppermute | solution.py:93
  224.3 18.2 %shard_map.299 = (f32[512,128]{1,0:T(8,128)}, bf16[320,2048]{1,0:T(8,128)(2,1)}, bf16[320,2816]{1,0:T(8,128)(2,1)}, bf16[320,1408]{1,0:T(8,128)(2,1)}, bf16[320,...) custom-call(bf16[4,80,128]{2,1,0:T(8,128)(2,1)} %get-tuple-element.6, ...), custom_call_target="tpu_custom_call" | custom-call | flops 7683964928 | bytes 35291136 | tf_op jit(solution)/shard_map/pallas_call | solution.py:335
  251.1 18.3 %shard_map.300 = (f32[512,128]{1,0:T(8,128)}, bf16[320,2048]{1,0:T(8,128)(2,1)}, bf16[320,2816]{1,0:T(8,128)(2,1)}, bf16[320,1408]{1,0:T(8,128)(2,1)}, bf16[320,...) custom-call(bf16[4,80,128]{2,1,0:T(8,128)(2,1)} %get-tuple-element.6, ...), custom_call_target="tpu_custom_call" | custom-call | flops 7683964928 | bytes 35291136 | tf_op jit(solution)/shard_map/pallas_call | solution.py:335
  276.1 9.4 %collective-permute-done.40 = bf16[1,128,2048]{2,1,0:T(8,128)(2,1)} collective-permute-done((bf16[1,128,2048]{2,1,0:T(8,128)(2,1)}, bf16[1,128,2048]{2,1,0:T(8,128)(2,1)}, u32[]{:S(2)}, u32[]{:S(2)}) %collective-permute-start.40) | collective-permute-done | bytes 524320 | tf_op jit(solution)/shard_map/ppermute | solution.py:93
  294.2 18.5 %shard_map.301 = (f32[512,128]{1,0:T(8,128)}, bf16[320,2048]{1,0:T(8,128)(2,1)}, bf16[320,2816]{1,0:T(8,128)(2,1)}, bf16[320,1408]{1,0:T(8,128)(2,1)}, bf16[320,...) custom-call(bf16[4,80,128]{2,1,0:T(8,128)(2,1)} %get-tuple-element.6, ...), custom_call_target="tpu_custom_call" | custom-call | flops 7683964928 | bytes 35291136 | tf_op jit(solution)/shard_map/pallas_call | solution.py:335
  312.8 10.3 %collective-permute-done.42 = bf16[2,128,2048]{2,1,0:T(8,128)(2,1)S(1)} collective-permute-done((bf16[2,128,2048]{2,1,0:T(8,128)(2,1)}, bf16[2,128,2048]{2,1,0:T(8,128)(2,1)S(1)}, u32[]{:S(2)}, u32[]{:S(2)}) %collective-permute-start.42) | collective-permute-done | bytes 1048608 | tf_op jit(solution)/shard_map/ppermute | solution.py:93
  325.0 3.9 collective-permute-done.45
  337.1 18.1 %shard_map.302 = (f32[512,128]{1,0:T(8,128)}, bf16[320,2048]{1,0:T(8,128)(2,1)}, bf16[320,2816]{1,0:T(8,128)(2,1)}, bf16[320,1408]{1,0:T(8,128)(2,1)}, bf16[320,...) custom-call(bf16[4,80,128]{2,1,0:T(8,128)(2,1)} %get-tuple-element.6, ...), custom_call_target="tpu_custom_call" | custom-call | flops 7683964928 | bytes 35291136 | tf_op jit(solution)/shard_map/pallas_call | solution.py:335
  362.3 9.6 %collective-permute-done.50 = bf16[1,128,2048]{2,1,0:T(8,128)(2,1)S(1)} collective-permute-done((bf16[1,128,2048]{2,1,0:T(8,128)(2,1)S(1)}, bf16[1,128,2048]{2,1,0:T(8,128)(2,1)S(1)}, u32[]{:S(2)}, u32[]{:S(2)}) %collective-permute-start.50) | collective-permute-done | bytes 524320 | tf_op jit(solution)/shard_map/ppermute | solution.py:93
  371.9 11.0 %collective-permute-done.51 = bf16[1,128,2048]{2,1,0:T(8,128)(2,1)S(1)} collective-permute-done((bf16[1,128,2048]{2,1,0:T(8,128)(2,1)S(1)}, bf16[1,128,2048]{2,1,0:T(8,128)(2,1)S(1)}, u32[]{:S(2)}, u32[]{:S(2)}) %collective-permute-start.51) | collective-permute-done | bytes 524320 | tf_op jit(solution)/shard_map/ppermute | solution.py:93
  383.3 11.8 %collective-permute-done.54 = bf16[128,2048]{1,0:T(8,128)(2,1)S(1)} collective-permute-done((bf16[128,2048]{1,0:T(8,128)(2,1)S(1)}, bf16[128,2048]{1,0:T(8,128)(2,1)S(1)}, u32[]{:S(2)}, u32[]{:S(2)}) %collective-permute-start.54) | collective-permute-done | bytes 524320 | tf_op jit(solution)/shard_map/ppermute | solution.py:93
  401.6 8.3 collective-permute-done.57.piece_2
  409.8 4.7 collective-permute-done.56.piece_1
  414.6 8.5 %collective-permute-done.58.piece_3 = bf16[1,128,2048]{2,1,0:T(8,128)(2,1)S(1)} collective-permute-done((bf16[1,128,2048]{2,1,0:T(8,128)(2,1)}, bf16[1,128,2048]{2,1,0:T(8,128)(2,1)S(1)}, u32[]{:S(2)}, u32[]{:S(2)}) %collective-permute-start.58) | collective-permute-done | bytes 524320 | tf_op jit(solution)/shard_map/ppermute | solution.py:93
  429.3 18.0 %shard_map.303 = (f32[512,128]{1,0:T(8,128)}, bf16[320,2048]{1,0:T(8,128)(2,1)}, bf16[320,2816]{1,0:T(8,128)(2,1)}, bf16[512,512]{1,0:T(8,128)(2,1)}, f32[1,128,...) custom-call(bf16[4,80,128]{2,1,0:T(8,128)(2,1)} %get-tuple-element.6, ...), custom_call_target="tpu_custom_call" | custom-call | flops 7683964928 | bytes 39485440 | tf_op jit(solution)/shard_map/pallas_call | solution.py:438
  447.4 4.3 collective-permute-done.62.piece_3
  451.7 2.9 pad_maximum_fusion.9
  458.9 18.1 %shard_map.304 = (f32[512,128]{1,0:T(8,128)}, bf16[320,2048]{1,0:T(8,128)(2,1)}, bf16[320,2816]{1,0:T(8,128)(2,1)}, bf16[512,512]{1,0:T(8,128)(2,1)}, f32[1,128,...) custom-call(bf16[4,80,128]{2,1,0:T(8,128)(2,1)} %get-tuple-element.6, ...), custom_call_target="tpu_custom_call" | custom-call | flops 7683964928 | bytes 39485440 | tf_op jit(solution)/shard_map/pallas_call | solution.py:438
  477.0 3.5 collective-permute-done.65
  484.7 8.9 %collective-permute-done.68 = bf16[1,128,2048]{2,1,0:T(8,128)(2,1)S(1)} collective-permute-done((bf16[1,128,2048]{2,1,0:T(8,128)(2,1)}, bf16[1,128,2048]{2,1,0:T(8,128)(2,1)S(1)}, u32[]{:S(2)}, u32[]{:S(2)}) %collective-permute-start.68) | collective-permute-done | bytes 524320 | tf_op jit(solution)/shard_map/ppermute | solution.py:93
  502.6 18.2 %shard_map.305 = (f32[512,128]{1,0:T(8,128)}, bf16[320,2048]{1,0:T(8,128)(2,1)}, bf16[320,2816]{1,0:T(8,128)(2,1)}, bf16[512,512]{1,0:T(8,128)(2,1)}, f32[1,128,...) custom-call(bf16[4,80,128]{2,1,0:T(8,128)(2,1)} %get-tuple-element.6, ...), custom_call_target="tpu_custom_call" | custom-call | flops 7683964928 | bytes 39485440 | tf_op jit(solution)/shard_map/pallas_call | solution.py:438
  521.8 9.2 %collective-permute-done.70 = bf16[2,128,2048]{2,1,0:T(8,128)(2,1)S(1)} collective-permute-done((bf16[2,128,2048]{2,1,0:T(8,128)(2,1)}, bf16[2,128,2048]{2,1,0:T(8,128)(2,1)S(1)}, u32[]{:S(2)}, u32[]{:S(2)}) %collective-permute-start.70) | collective-permute-done | bytes 1048608 | tf_op jit(solution)/shard_map/ppermute | solution.py:93
  533.5 3.3 collective-permute-done.73
  545.2 18.1 %shard_map.306 = (f32[512,128]{1,0:T(8,128)}, bf16[320,2048]{1,0:T(8,128)(2,1)}, bf16[320,2816]{1,0:T(8,128)(2,1)}, bf16[512,512]{1,0:T(8,128)(2,1)}, f32[1,128,...) custom-call(bf16[4,80,128]{2,1,0:T(8,128)(2,1)} %get-tuple-element.6, ...), custom_call_target="tpu_custom_call" | custom-call | flops 7683964928 | bytes 39485440 | tf_op jit(solution)/shard_map/pallas_call | solution.py:438
  572.3 7.1 shard_map.308
  579.4 9.4 %shard_map.307 = f32[2048,512]{1,0:T(8,128)} custom-call(bf16[128,2048]{1,0:T(8,128)(2,1)} %bitcast.88.refs_0_, bf16[128,2048]{1,0:T(8,128)(2,1)} %bitcast.89.refs_1_, bf16[128,2048]{1,0:T(8,128)(2,1)} %bitcast.90.refs_2_, bf16[128,2048]{1,0:T(8,128)(2,1)} %bitcast.91.refs_3_, bf16[128,2048]{1,0:T(8,128)(2,1)} %bitcast.92.refs_4_, ...), custom_call_target="tpu_custom_call" | custom-call | flops 4294967296 | bytes 14680064 | tf_op jit(solution)/shard_map/pallas_call | solution.py:188
  590.5 2.7 add_add_fusion.1
  594.5 3.6 all-to-all-start.2
  600.2 13.7 %shard_map.309 = f32[1408,2048]{1,0:T(8,128)} custom-call(bf16[320,1408]{1,0:T(8,128)(2,1)} %get-tuple-element.435.refs_0_, bf16[320,1408]{1,0:T(8,128)(2,1)} %get-tuple-element.436.refs_1_, bf16[320,1408]{1,0:T(8,128)(2,1)} %get-tuple-element.437.refs_2_, bf16[320,1408]{1,0:T(8,128)(2,1)} %get-tuple-element.438.refs_3_, ...), custom_call_target="tpu_custom_call" | custom-call | flops 7381975040 | bytes 20381696 | tf_op jit(solution)/shard_map/pallas_call | solution.py:188
  616.3 3.2 multiply_reduce_fusion
  628.1 6.1 all-to-all-start.3
  634.2 24.3 %shard_map.310 = f32[2048,2816]{1,0:T(8,128)} custom-call(bf16[320,2048]{1,0:T(8,128)(2,1)} %get-tuple-element.450.refs_0_, bf16[320,2048]{1,0:T(8,128)(2,1)} %get-tuple-element.451.refs_1_, bf16[320,2048]{1,0:T(8,128)(2,1)} %get-tuple-element.452.refs_2_, bf16[320,2048]{1,0:T(8,128)(2,1)} %get-tuple-element.453.refs_3_, ...), custom_call_target="tpu_custom_call" | custom-call | flops 14763950080 | bytes 35520512 | tf_op jit(solution)/shard_map/pallas_call | solution.py:188
  663.2 4.0 collective-permute-done.87.away_ref
  668.6 5.7 shard_map.311
  680.9 20.7 %shard_map.312 = (bf16[2048,384]{1,0:T(8,128)(2,1)}, bf16[512,512]{1,0:T(8,128)(2,1)}, bf16[4,128,2688]{2,1,0:T(8,128)(2,1)}, bf16[4,128,2688]{2,1,0:T(8,128)(2,1)}) custom-call(bf16[4,128,2048]{2,1,0:T(8,128)(2,1)} %copy-done.2, bf16[4,128,2048]{2,1,0:T(8,128)(2,1)} %copy-done.18, bf16[1024,384]{1,0:T(8,128)(2,1)} %get-tuple-element.461.queries_ref, ...), custom_call_target="tpu_custom_call" | custom-call | flops 6442450944 | bytes 50331648 | tf_op jit(solution)/shard_map/pallas_call | solution.py:633
  723.0 4.7 all-to-all-start.4
  727.8 5.0 collective-permute-done.92
  732.8 15.1 %collective-permute-done.93 = bf16[128,2688]{1,0:T(8,128)(2,1)} collective-permute-done((bf16[128,2688]{1,0:T(8,128)(2,1)}, bf16[128,2688]{1,0:T(8,128)(2,1)}, u32[]{:S(2)}, u32[]{:S(2)}) %collective-permute-start.93) | collective-permute-done | bytes 688160 | tf_op jit(solution)/shard_map/ppermute | solution.py:93
  754.5 4.1 fusion.10
  758.6 4.3 add_convert_fusion.1
  762.9 2.9 gather_fusion.9
  777.2 2.9 reduce_sum.156
  780.1 4.3 all-to-all-start.5
  788.9 2.7 fusion.7
  791.7 3.6 collective-permute-start.99
  795.3 3.7 reshape.628
  798.9 2.8 copy.256
  804.9 11.6 %collective-permute-done.98 = bf16[4,64,640]{2,1,0:T(8,128)(2,1)} collective-permute-done((bf16[4,64,640]{2,1,0:T(8,128)(2,1)}, bf16[4,64,640]{2,1,0:T(8,128)(2,1)}, u32[]{:S(2)}, u32[]{:S(2)}) %collective-permute-start.98) | collective-permute-done | bytes 327712 | tf_op jit(solution)/shard_map/ppermute | solution.py:93
  821.6 5.7 collective-permute-start.102
  832.2 2.8 collective-permute-done.101
  (591 shorter events, 292.1 us)
Async XLA Ops:
  7.3 217.0 %all-gather.5.cloned.1.call-start = ((), (), s32[]{:S(2)}) async-start(), calls=%async_computation.11 | async-start | bytes 8650752 | tf_op jit(solution)/shard_map/all_gather | solution.py:790
  8.2 31.7 %collective-permute-start.3 = (bf16[128,2048]{1,0:T(8,128)(2,1)S(1)}, bf16[128,2048]{1,0:T(8,128)(2,1)}, u32[]{:S(2)}, u32[]{:S(2)}) collective-permute-start(bf16[128,2048]{1,0:T(8,128)(2,1)S(1)} %bitcast.312), channel_id=1, source_target_pairs={{0,1},{1,0},{2,3},{3,2},{4,5},{5,4},{6,7},{7,6},{8,9},{9,8},{10,11... | collective-permute-start | bytes 1572872 | tf_op jit(solution)/shard_map/ppermute | solution.py:93
  11.2 28.8 %collective-permute-start.5 = (bf16[128,2048]{1,0:T(8,128)(2,1)S(1)}, bf16[128,2048]{1,0:T(8,128)(2,1)}, u32[]{:S(2)}, u32[]{:S(2)}) collective-permute-start(bf16[128,2048]{1,0:T(8,128)(2,1)S(1)} %bitcast.313), channel_id=1, source_target_pairs={{0,3},{1,2},{2,1},{3,0},{4,7},{5,6},{6,5},{7,4},{8,11},{9,10},{10,... | collective-permute-start | bytes 1572872 | tf_op jit(solution)/shard_map/ppermute | solution.py:93
  12.7 27.3 %collective-permute-start.4 = (bf16[128,2048]{1,0:T(8,128)(2,1)S(1)}, bf16[128,2048]{1,0:T(8,128)(2,1)}, u32[]{:S(2)}, u32[]{:S(2)}) collective-permute-start(bf16[128,2048]{1,0:T(8,128)(2,1)S(1)} %bitcast.314), channel_id=1, source_target_pairs={{0,2},{1,3},{2,0},{3,1},{4,6},{5,7},{6,4},{7,5},{8,10},{9,11},{10,... | collective-permute-start | bytes 1572872 | tf_op jit(solution)/shard_map/ppermute | solution.py:93
  21.9 23.6 %all-to-all-start = ((bf16[8,64,512]{2,1,0:T(8,128)(2,1)}), bf16[8,64,512]{2,1,0:T(8,128)(2,1)}, u32[]{:S(2)}, u32[]{:S(2)}) async-start(bf16[8,64,512]{2,1,0:T(8,128)(2,1)} %maximum_bitcast_fusion), calls=%async_computation | async-start | bytes 1048576 | tf_op jit(solution)/shard_map/all_to_all | solution.py:724
  26.1 198.2 %all-gather.3.cloned.1.call-start = ((), (), s32[]{:S(2)}) async-start(), calls=%async_computation.10 | async-start | bytes 17301504 | tf_op jit(solution)/shard_map/all_gather | solution.py:789
  31.1 77.4 %collective-permute-start.14 = (bf16[64,2048]{1,0:T(8,128)(2,1)}, bf16[64,2048]{1,0:T(8,128)(2,1)}, u32[]{:S(2)}, u32[]{:S(2)}) collective-permute-start(bf16[64,2048]{1,0:T(8,128)(2,1)} %param.25), channel_id=1, source_target_pairs={{0,0},{1,4},{2,8},{3,12},{4,1},{5,5},{6,9},{7,13},{8,2},{9,6},{10,... | collective-permute-start | bytes 786440 | tf_op jit(solution)/shard_map/ppermute | solution.py:708
  53.0 55.9 %all-to-all-start.1 = ((bf16[4,2,256,512]{3,2,1,0:T(8,128)(2,1)}), bf16[4,2,256,512]{3,2,1,0:T(8,128)(2,1)}, u32[]{:S(2)}, u32[]{:S(2)}) async-start(bf16[4,2,256,512]{3,2,1,0:T(8,128)(2,1)} %broadcast_in_dim.172), calls=%async_computation.1 | async-start | bytes 4194304 | tf_op jit(solution)/shard_map/all_to_all | solution.py:133
  61.1 563.7 %reduce-scatter.5.cloned.1.call-start = ((), (), s32[]{:S(2)}) async-start(), calls=%async_computation.12 | async-start | bytes 6291456 | tf_op jit(solution)/shard_map/reduce_scatter | solution.py:977
  83.8 24.8 %collective-permute-start.6 = (bf16[4,128,2048]{2,1,0:T(8,128)(2,1)}, bf16[4,128,2048]{2,1,0:T(8,128)(2,1)}, u32[]{:S(2)}, u32[]{:S(2)}) collective-permute-start(bf16[4,128,2048]{2,1,0:T(8,128)(2,1)} %pad_maximum_fusion.1.near_ref), channel_id=1, source_target_pairs={{0,16},{16,0},{1,17},{17,1},{2,18},{18,2},{3,19},{19,3},{4,20},{20... | collective-permute-start | bytes 6291464 | tf_op jit(solution)/shard_map/ppermute | solution.py:93
  108.9 30.1 %collective-permute-start.16 = (bf16[64,2048]{1,0:T(8,128)(2,1)}, bf16[64,2048]{1,0:T(8,128)(2,1)S(1)}, u32[]{:S(2)}, u32[]{:S(2)}) collective-permute-start(bf16[64,2048]{1,0:T(8,128)(2,1)} %collective-permute-done.14), channel_id=1, source_target_pairs={{0,8},{4,12},{8,0},{12,4},{1,9},{5,13},{9,1},{13,5},{2,10},{6,14},... | collective-permute-start | bytes 786440 | tf_op jit(solution)/shard_map/ppermute | solution.py:93
  110.6 28.4 %collective-permute-start.15 = (bf16[64,2048]{1,0:T(8,128)(2,1)}, bf16[64,2048]{1,0:T(8,128)(2,1)}, u32[]{:S(2)}, u32[]{:S(2)}) collective-permute-start(bf16[64,2048]{1,0:T(8,128)(2,1)} %collective-permute-done.14), channel_id=1, source_target_pairs={{0,4},{4,0},{8,12},{12,8},{1,5},{5,1},{9,13},{13,9},{2,6},{6,2},{1... | collective-permute-start | bytes 786440 | tf_op jit(solution)/shard_map/ppermute | solution.py:93
  113.1 25.9 %collective-permute-start.17 = (bf16[64,2048]{1,0:T(8,128)(2,1)}, bf16[64,2048]{1,0:T(8,128)(2,1)}, u32[]{:S(2)}, u32[]{:S(2)}) collective-permute-start(bf16[64,2048]{1,0:T(8,128)(2,1)} %collective-permute-done.14), channel_id=1, source_target_pairs={{0,12},{4,8},{8,4},{12,0},{1,13},{5,9},{9,5},{13,1},{2,14},{6,10},... | collective-permute-start | bytes 786440 | tf_op jit(solution)/shard_map/ppermute | solution.py:93
  159.5 25.5 %collective-permute-start.21 = (bf16[128,2048]{1,0:T(8,128)(2,1)}, bf16[128,2048]{1,0:T(8,128)(2,1)}, u32[]{:S(2)}, u32[]{:S(2)}) collective-permute-start(bf16[128,2048]{1,0:T(8,128)(2,1)} %get-tuple-element.619), channel_id=1, source_target_pairs={{0,2},{1,3},{2,0},{3,1},{4,6},{5,7},{6,4},{7,5},{8,10},{9,11},{10,... | collective-permute-start | bytes 1572872 | tf_op jit(solution)/shard_map/ppermute | solution.py:93
  160.4 24.6 %collective-permute-start.22 = (bf16[128,2048]{1,0:T(8,128)(2,1)}, bf16[128,2048]{1,0:T(8,128)(2,1)}, u32[]{:S(2)}, u32[]{:S(2)}) collective-permute-start(bf16[128,2048]{1,0:T(8,128)(2,1)} %get-tuple-element.620), channel_id=1, source_target_pairs={{0,3},{1,2},{2,1},{3,0},{4,7},{5,6},{6,5},{7,4},{8,11},{9,10},{10,... | collective-permute-start | bytes 1572872 | tf_op jit(solution)/shard_map/ppermute | solution.py:93
  190.1 28.4 %collective-permute-start.28 = (bf16[1,128,2048]{2,1,0:T(8,128)(2,1)}, bf16[1,128,2048]{2,1,0:T(8,128)(2,1)}, u32[]{:S(2)}, u32[]{:S(2)}) collective-permute-start(bf16[1,128,2048]{2,1,0:T(8,128)(2,1)} %fusion.55.piece_0), channel_id=1, source_target_pairs={{0,2},{1,3},{2,0},{3,1},{4,6},{5,7},{6,4},{7,5},{8,10},{9,11},{10,... | collective-permute-start | bytes 1572872 | tf_op jit(solution)/shard_map/ppermute | solution.py:93
  191.6 26.9 %collective-permute-start.27 = (bf16[1,128,2048]{2,1,0:T(8,128)(2,1)}, bf16[1,128,2048]{2,1,0:T(8,128)(2,1)}, u32[]{:S(2)}, u32[]{:S(2)}) collective-permute-start(bf16[1,128,2048]{2,1,0:T(8,128)(2,1)} %fusion.55.piece_0), channel_id=1, source_target_pairs={{0,1},{1,0},{2,3},{3,2},{4,5},{5,4},{6,7},{7,6},{8,9},{9,8},{10,11... | collective-permute-start | bytes 1572872 | tf_op jit(solution)/shard_map/ppermute | solution.py:93
  192.1 26.4 %collective-permute-start.29 = (bf16[1,128,2048]{2,1,0:T(8,128)(2,1)}, bf16[1,128,2048]{2,1,0:T(8,128)(2,1)}, u32[]{:S(2)}, u32[]{:S(2)}) collective-permute-start(bf16[1,128,2048]{2,1,0:T(8,128)(2,1)} %fusion.55.piece_0), channel_id=1, source_target_pairs={{0,3},{1,2},{2,1},{3,0},{4,7},{5,6},{6,5},{7,4},{8,11},{9,10},{10,... | collective-permute-start | bytes 1572872 | tf_op jit(solution)/shard_map/ppermute | solution.py:93
  193.8 24.7 %collective-permute-start.26 = (bf16[128,2048]{1,0:T(8,128)(2,1)S(1)}, bf16[128,2048]{1,0:T(8,128)(2,1)}, u32[]{:S(2)}, u32[]{:S(2)}) collective-permute-start(bf16[128,2048]{1,0:T(8,128)(2,1)S(1)} %multiply_convert_fusion), channel_id=1, source_target_pairs={{0,8},{4,12},{8,0},{12,4},{1,9},{5,13},{9,1},{13,5},{2,10},{6,14},... | collective-permute-start | bytes 1572872 | tf_op jit(solution)/shard_map/ppermute | solution.py:93
  218.5 24.0 %collective-permute-start.33 = (bf16[1,128,2048]{2,1,0:T(8,128)(2,1)}, bf16[1,128,2048]{2,1,0:T(8,128)(2,1)S(1)}, u32[]{:S(2)}, u32[]{:S(2)}) collective-permute-start(bf16[1,128,2048]{2,1,0:T(8,128)(2,1)} %bitcast.59.piece_0), channel_id=1, source_target_pairs={{0,2},{1,3},{2,0},{3,1},{4,6},{5,7},{6,4},{7,5},{8,10},{9,11},{10,... | collective-permute-start | bytes 1572872 | tf_op jit(solution)/shard_map/ppermute | solution.py:93
  220.4 24.7 %collective-permute-start.34 = (bf16[1,128,2048]{2,1,0:T(8,128)(2,1)}, bf16[1,128,2048]{2,1,0:T(8,128)(2,1)}, u32[]{:S(2)}, u32[]{:S(2)}) collective-permute-start(bf16[1,128,2048]{2,1,0:T(8,128)(2,1)} %bitcast.59.piece_0), channel_id=1, source_target_pairs={{0,3},{1,2},{2,1},{3,0},{4,7},{5,6},{6,5},{7,4},{8,11},{9,10},{10,... | collective-permute-start | bytes 1572872 | tf_op jit(solution)/shard_map/ppermute | solution.py:93
  246.5 25.3 %collective-permute-start.37 = (bf16[2,128,2048]{2,1,0:T(8,128)(2,1)S(1)}, bf16[2,128,2048]{2,1,0:T(8,128)(2,1)S(1)}, u32[]{:S(2)}, u32[]{:S(2)}) collective-permute-start(bf16[2,128,2048]{2,1,0:T(8,128)(2,1)S(1)} %get-tuple-element.671), channel_id=1, source_target_pairs={{0,2},{1,3},{2,0},{3,1},{4,6},{5,7},{6,4},{7,5},{8,10},{9,11},{10,... | collective-permute-start | bytes 3145736 | tf_op jit(solution)/shard_map/ppermute | solution.py:93
  248.2 26.1 %collective-permute-start.36 = (bf16[2,128,2048]{2,1,0:T(8,128)(2,1)S(1)}, bf16[2,128,2048]{2,1,0:T(8,128)(2,1)S(1)}, u32[]{:S(2)}, u32[]{:S(2)}) collective-permute-start(bf16[2,128,2048]{2,1,0:T(8,128)(2,1)S(1)} %get-tuple-element.672), channel_id=1, source_target_pairs={{0,1},{1,0},{2,3},{3,2},{4,5},{5,4},{6,7},{7,6},{8,9},{9,8},{10,11... | collective-permute-start | bytes 3145736 | tf_op jit(solution)/shard_map/ppermute | solution.py:93
  248.5 37.0 %collective-permute-start.40 = (bf16[1,128,2048]{2,1,0:T(8,128)(2,1)}, bf16[1,128,2048]{2,1,0:T(8,128)(2,1)}, u32[]{:S(2)}, u32[]{:S(2)}) collective-permute-start(bf16[1,128,2048]{2,1,0:T(8,128)(2,1)} %get-tuple-element.303), channel_id=1, source_target_pairs={{0,3},{1,2},{2,1},{3,0},{4,7},{5,6},{6,5},{7,4},{8,11},{9,10},{10,... | collective-permute-start | bytes 1572872 | tf_op jit(solution)/shard_map/ppermute | solution.py:93
  250.1 39.5 %collective-permute-start.35 = (bf16[128,2048]{1,0:T(8,128)(2,1)S(1)}, bf16[128,2048]{1,0:T(8,128)(2,1)S(1)}, u32[]{:S(2)}, u32[]{:S(2)}) collective-permute-start(bf16[128,2048]{1,0:T(8,128)(2,1)S(1)} %multiply_convert_fusion), channel_id=1, source_target_pairs={{0,4},{4,0},{8,12},{12,8},{1,5},{5,1},{9,13},{13,9},{2,6},{6,2},{1... | collective-permute-start | bytes 1572872 | tf_op jit(solution)/shard_map/ppermute | solution.py:93
  290.8 32.4 %collective-permute-start.42 = (bf16[2,128,2048]{2,1,0:T(8,128)(2,1)}, bf16[2,128,2048]{2,1,0:T(8,128)(2,1)S(1)}, u32[]{:S(2)}, u32[]{:S(2)}) collective-permute-start(bf16[2,128,2048]{2,1,0:T(8,128)(2,1)} %get-tuple-element.669), channel_id=1, source_target_pairs={{0,2},{1,3},{2,0},{3,1},{4,6},{5,7},{6,4},{7,5},{8,10},{9,11},{10,... | collective-permute-start | bytes 3145736 | tf_op jit(solution)/shard_map/ppermute | solution.py:93
  292.2 30.9 %collective-permute-start.41 = (bf16[2,128,2048]{2,1,0:T(8,128)(2,1)S(1)}, bf16[2,128,2048]{2,1,0:T(8,128)(2,1)S(1)}, u32[]{:S(2)}, u32[]{:S(2)}) collective-permute-start(bf16[2,128,2048]{2,1,0:T(8,128)(2,1)S(1)} %get-tuple-element.670), channel_id=1, source_target_pairs={{0,1},{1,0},{2,3},{3,2},{4,5},{5,4},{6,7},{7,6},{8,9},{9,8},{10,11... | collective-permute-start | bytes 3145736 | tf_op jit(solution)/shard_map/ppermute | solution.py:93
  292.5 36.4 %collective-permute-start.45 = (bf16[1,128,2048]{2,1,0:T(8,128)(2,1)}, bf16[1,128,2048]{2,1,0:T(8,128)(2,1)S(1)}, u32[]{:S(2)}, u32[]{:S(2)}) collective-permute-start(bf16[1,128,2048]{2,1,0:T(8,128)(2,1)} %get-tuple-element.318), channel_id=1, source_target_pairs={{0,3},{1,2},{2,1},{3,0},{4,7},{5,6},{6,5},{7,4},{8,11},{9,10},{10,... | collective-permute-start | bytes 1572872 | tf_op jit(solution)/shard_map/ppermute | solution.py:93
  332.3 23.0 %collective-permute-start.46 = (bf16[1,128,2048]{2,1,0:T(8,128)(2,1)}, bf16[1,128,2048]{2,1,0:T(8,128)(2,1)S(1)}, u32[]{:S(2)}, u32[]{:S(2)}) collective-permute-start(bf16[1,128,2048]{2,1,0:T(8,128)(2,1)} %get-tuple-element.330), channel_id=1, source_target_pairs={{0,1},{1,0},{2,3},{3,2},{4,5},{5,4},{6,7},{7,6},{8,9},{9,8},{10,11... | collective-permute-start | bytes 1572872 | tf_op jit(solution)/shard_map/ppermute | solution.py:93
  358.1 24.8 %collective-permute-start.51 = (bf16[1,128,2048]{2,1,0:T(8,128)(2,1)S(1)}, bf16[1,128,2048]{2,1,0:T(8,128)(2,1)S(1)}, u32[]{:S(2)}, u32[]{:S(2)}) collective-permute-start(bf16[1,128,2048]{2,1,0:T(8,128)(2,1)S(1)} %copy-done.87), channel_id=1, source_target_pairs={{0,2},{1,3},{2,0},{3,1},{4,6},{5,7},{6,4},{7,5},{8,10},{9,11},{10,... | collective-permute-start | bytes 1572872 | tf_op jit(solution)/shard_map/ppermute | solution.py:93
  359.3 23.6 %collective-permute-start.52 = (bf16[1,128,2048]{2,1,0:T(8,128)(2,1)S(1)}, bf16[1,128,2048]{2,1,0:T(8,128)(2,1)S(1)}, u32[]{:S(2)}, u32[]{:S(2)}) collective-permute-start(bf16[1,128,2048]{2,1,0:T(8,128)(2,1)S(1)} %copy-done.86), channel_id=1, source_target_pairs={{0,3},{1,2},{2,1},{3,0},{4,7},{5,6},{6,5},{7,4},{8,11},{9,10},{10,... | collective-permute-start | bytes 1572872 | tf_op jit(solution)/shard_map/ppermute | solution.py:93
  360.6 22.6 %collective-permute-start.53 = (bf16[128,2048]{1,0:T(8,128)(2,1)S(1)}, bf16[128,2048]{1,0:T(8,128)(2,1)S(1)}, u32[]{:S(2)}, u32[]{:S(2)}) collective-permute-start(bf16[128,2048]{1,0:T(8,128)(2,1)S(1)} %bitcast.379), channel_id=1, source_target_pairs={{0,12},{4,8},{8,4},{12,0},{1,13},{5,9},{9,5},{13,1},{2,14},{6,10},... | collective-permute-start | bytes 1572872 | tf_op jit(solution)/shard_map/ppermute | solution.py:93
  401.6 23.9 %collective-permute-start.55 = (bf16[128,2048]{1,0:T(8,128)(2,1)}, bf16[128,2048]{1,0:T(8,128)(2,1)S(1)}, u32[]{:S(2)}, u32[]{:S(2)}) collective-permute-start(bf16[128,2048]{1,0:T(8,128)(2,1)} %fusion.24), channel_id=1, source_target_pairs={{0,8},{4,12},{8,0},{12,4},{1,9},{5,13},{9,1},{13,5},{2,10},{6,14},... | collective-permute-start | bytes 1572872 | tf_op jit(solution)/shard_map/ppermute | solution.py:93
  427.8 23.9 %collective-permute-start.62 = (bf16[1,128,2048]{2,1,0:T(8,128)(2,1)S(1)}, bf16[1,128,2048]{2,1,0:T(8,128)(2,1)S(1)}, u32[]{:S(2)}, u32[]{:S(2)}) collective-permute-start(bf16[1,128,2048]{2,1,0:T(8,128)(2,1)S(1)} %bitcast.363), channel_id=1, source_target_pairs={{0,3},{1,2},{2,1},{3,0},{4,7},{5,6},{6,5},{7,4},{8,11},{9,10},{10,... | collective-permute-start | bytes 1572872 | tf_op jit(solution)/shard_map/ppermute | solution.py:93
  454.6 25.9 %collective-permute-start.65 = (bf16[2,128,2048]{2,1,0:T(8,128)(2,1)}, bf16[2,128,2048]{2,1,0:T(8,128)(2,1)S(1)}, u32[]{:S(2)}, u32[]{:S(2)}) collective-permute-start(bf16[2,128,2048]{2,1,0:T(8,128)(2,1)} %get-tuple-element.667), channel_id=1, source_target_pairs={{0,2},{1,3},{2,0},{3,1},{4,6},{5,7},{6,4},{7,5},{8,10},{9,11},{10,... | collective-permute-start | bytes 3145736 | tf_op jit(solution)/shard_map/ppermute | solution.py:93
  455.2 26.3 %collective-permute-start.64 = (bf16[2,128,2048]{2,1,0:T(8,128)(2,1)}, bf16[2,128,2048]{2,1,0:T(8,128)(2,1)S(1)}, u32[]{:S(2)}, u32[]{:S(2)}) collective-permute-start(bf16[2,128,2048]{2,1,0:T(8,128)(2,1)} %get-tuple-element.668), channel_id=1, source_target_pairs={{0,1},{1,0},{2,3},{3,2},{4,5},{5,4},{6,7},{7,6},{8,9},{9,8},{10,11... | collective-permute-start | bytes 3145736 | tf_op jit(solution)/shard_map/ppermute | solution.py:93
  456.9 36.7 %collective-permute-start.68 = (bf16[1,128,2048]{2,1,0:T(8,128)(2,1)}, bf16[1,128,2048]{2,1,0:T(8,128)(2,1)S(1)}, u32[]{:S(2)}, u32[]{:S(2)}) collective-permute-start(bf16[1,128,2048]{2,1,0:T(8,128)(2,1)} %get-tuple-element.376), channel_id=1, source_target_pairs={{0,3},{1,2},{2,1},{3,0},{4,7},{5,6},{6,5},{7,4},{8,11},{9,10},{10,... | collective-permute-start | bytes 1572872 | tf_op jit(solution)/shard_map/ppermute | solution.py:93
  458.1 39.3 %collective-permute-start.63 = (bf16[128,2048]{1,0:T(8,128)(2,1)}, bf16[128,2048]{1,0:T(8,128)(2,1)S(1)}, u32[]{:S(2)}, u32[]{:S(2)}) collective-permute-start(bf16[128,2048]{1,0:T(8,128)(2,1)} %fusion.24), channel_id=1, source_target_pairs={{0,4},{4,0},{8,12},{12,8},{1,5},{5,1},{9,13},{13,9},{2,6},{6,2},{1... | collective-permute-start | bytes 1572872 | tf_op jit(solution)/shard_map/ppermute | solution.py:93
  498.7 32.3 %collective-permute-start.70 = (bf16[2,128,2048]{2,1,0:T(8,128)(2,1)}, bf16[2,128,2048]{2,1,0:T(8,128)(2,1)S(1)}, u32[]{:S(2)}, u32[]{:S(2)}) collective-permute-start(bf16[2,128,2048]{2,1,0:T(8,128)(2,1)} %get-tuple-element.665), channel_id=1, source_target_pairs={{0,2},{1,3},{2,0},{3,1},{4,6},{5,7},{6,4},{7,5},{8,10},{9,11},{10,... | collective-permute-start | bytes 3145736 | tf_op jit(solution)/shard_map/ppermute | solution.py:93
  499.4 31.6 %collective-permute-start.69 = (bf16[2,128,2048]{2,1,0:T(8,128)(2,1)S(1)}, bf16[2,128,2048]{2,1,0:T(8,128)(2,1)S(1)}, u32[]{:S(2)}, u32[]{:S(2)}) collective-permute-start(bf16[2,128,2048]{2,1,0:T(8,128)(2,1)S(1)} %get-tuple-element.666), channel_id=1, source_target_pairs={{0,1},{1,0},{2,3},{3,2},{4,5},{5,4},{6,7},{7,6},{8,9},{9,8},{10,11... | collective-permute-start | bytes 3145736 | tf_op jit(solution)/shard_map/ppermute | solution.py:93
  501.5 35.3 %collective-permute-start.73 = (bf16[1,128,2048]{2,1,0:T(8,128)(2,1)}, bf16[1,128,2048]{2,1,0:T(8,128)(2,1)S(1)}, u32[]{:S(2)}, u32[]{:S(2)}) collective-permute-start(bf16[1,128,2048]{2,1,0:T(8,128)(2,1)} %get-tuple-element.395), channel_id=1, source_target_pairs={{0,3},{1,2},{2,1},{3,0},{4,7},{5,6},{6,5},{7,4},{8,11},{9,10},{10,... | collective-permute-start | bytes 1572872 | tf_op jit(solution)/shard_map/ppermute | solution.py:93
  539.8 24.7 %collective-permute-start.74 = (bf16[1,128,2048]{2,1,0:T(8,128)(2,1)}, bf16[1,128,2048]{2,1,0:T(8,128)(2,1)S(1)}, u32[]{:S(2)}, u32[]{:S(2)}) collective-permute-start(bf16[1,128,2048]{2,1,0:T(8,128)(2,1)} %get-tuple-element.409), channel_id=1, source_target_pairs={{0,1},{1,0},{2,3},{3,2},{4,5},{5,4},{6,7},{7,6},{8,9},{9,8},{10,11... | collective-permute-start | bytes 1572872 | tf_op jit(solution)/shard_map/ppermute | solution.py:93
  541.5 22.9 %collective-permute-start.75 = (bf16[1,128,2048]{2,1,0:T(8,128)(2,1)}, bf16[1,128,2048]{2,1,0:T(8,128)(2,1)S(1)}, u32[]{:S(2)}, u32[]{:S(2)}) collective-permute-start(bf16[1,128,2048]{2,1,0:T(8,128)(2,1)} %get-tuple-element.410), channel_id=1, source_target_pairs={{0,2},{1,3},{2,0},{3,1},{4,6},{5,7},{6,4},{7,5},{8,10},{9,11},{10,... | collective-permute-start | bytes 1572872 | tf_op jit(solution)/shard_map/ppermute | solution.py:93
  565.6 23.2 %collective-permute-start.78 = (bf16[1,128,2048]{2,1,0:T(8,128)(2,1)}, bf16[1,128,2048]{2,1,0:T(8,128)(2,1)}, u32[]{:S(2)}, u32[]{:S(2)}) collective-permute-start(bf16[1,128,2048]{2,1,0:T(8,128)(2,1)} %get-tuple-element.414), channel_id=1, source_target_pairs={{0,1},{1,0},{2,3},{3,2},{4,5},{5,4},{6,7},{7,6},{8,9},{9,8},{10,11... | collective-permute-start | bytes 1572872 | tf_op jit(solution)/shard_map/ppermute | solution.py:93
  567.6 22.9 %collective-permute-start.79 = (bf16[1,128,2048]{2,1,0:T(8,128)(2,1)}, bf16[1,128,2048]{2,1,0:T(8,128)(2,1)}, u32[]{:S(2)}, u32[]{:S(2)}) collective-permute-start(bf16[1,128,2048]{2,1,0:T(8,128)(2,1)} %get-tuple-element.415), channel_id=1, source_target_pairs={{0,2},{1,3},{2,0},{3,1},{4,6},{5,7},{6,4},{7,5},{8,10},{9,11},{10,... | collective-permute-start | bytes 1572872 | tf_op jit(solution)/shard_map/ppermute | solution.py:93
  568.1 22.4 %collective-permute-start.80 = (bf16[1,128,2048]{2,1,0:T(8,128)(2,1)}, bf16[1,128,2048]{2,1,0:T(8,128)(2,1)}, u32[]{:S(2)}, u32[]{:S(2)}) collective-permute-start(bf16[1,128,2048]{2,1,0:T(8,128)(2,1)} %get-tuple-element.416), channel_id=1, source_target_pairs={{0,3},{1,2},{2,1},{3,0},{4,7},{5,6},{6,5},{7,4},{8,11},{9,10},{10,... | collective-permute-start | bytes 1572872 | tf_op jit(solution)/shard_map/ppermute | solution.py:93
  569.1 24.2 %collective-permute-start.81 = (bf16[128,2048]{1,0:T(8,128)(2,1)}, bf16[128,2048]{1,0:T(8,128)(2,1)}, u32[]{:S(2)}, u32[]{:S(2)}) collective-permute-start(bf16[128,2048]{1,0:T(8,128)(2,1)} %bitcast.270), channel_id=1, source_target_pairs={{0,12},{4,8},{8,4},{12,0},{1,13},{5,9},{9,5},{13,1},{2,14},{6,10},... | collective-permute-start | bytes 1572872 | tf_op jit(solution)/shard_map/ppermute | solution.py:93
  593.3 179.1 %reduce-scatter.7.cloned.1.call-start = ((), (), s32[]{:S(2)}) async-start(), calls=%async_computation.13 | async-start | bytes 3145728 | tf_op jit(solution)/shard_map/reduce_scatter | solution.py:974
  598.1 239.1 %reduce-scatter.11.cloned.1.call-start = ((), (), s32[]{:S(2)}) async-start(), calls=%async_computation.15 | async-start | bytes 17301504 | tf_op jit(solution)/shard_map/reduce_scatter | solution.py:971
  621.3 37.2 %collective-permute-start.85 = (bf16[128,2048]{1,0:T(8,128)(2,1)}, bf16[128,2048]{1,0:T(8,128)(2,1)S(1)}, u32[]{:S(2)}, u32[]{:S(2)}) collective-permute-start(bf16[128,2048]{1,0:T(8,128)(2,1)} %get-tuple-element.609), channel_id=1, source_target_pairs={{0,2},{1,3},{2,0},{3,1},{4,6},{5,7},{6,4},{7,5},{8,10},{9,11},{10,... | collective-permute-start | bytes 1572872 | tf_op jit(solution)/shard_map/ppermute | solution.py:93
  622.8 35.8 %collective-permute-start.84 = (bf16[128,2048]{1,0:T(8,128)(2,1)}, bf16[128,2048]{1,0:T(8,128)(2,1)S(1)}, u32[]{:S(2)}, u32[]{:S(2)}) collective-permute-start(bf16[128,2048]{1,0:T(8,128)(2,1)} %get-tuple-element.609), channel_id=1, source_target_pairs={{0,1},{1,0},{2,3},{3,2},{4,5},{5,4},{6,7},{7,6},{8,9},{9,8},{10,11... | collective-permute-start | bytes 1572872 | tf_op jit(solution)/shard_map/ppermute | solution.py:93
  624.3 34.3 %collective-permute-start.86 = (bf16[128,2048]{1,0:T(8,128)(2,1)}, bf16[128,2048]{1,0:T(8,128)(2,1)S(1)}, u32[]{:S(2)}, u32[]{:S(2)}) collective-permute-start(bf16[128,2048]{1,0:T(8,128)(2,1)} %get-tuple-element.609), channel_id=1, source_target_pairs={{0,3},{1,2},{2,1},{3,0},{4,7},{5,6},{6,5},{7,4},{8,11},{9,10},{10,... | collective-permute-start | bytes 1572872 | tf_op jit(solution)/shard_map/ppermute | solution.py:93
  628.1 33.4 %all-to-all-start.3 = ((bf16[16,64,352]{2,1,0:T(8,128)(2,1)}), bf16[16,64,352]{2,1,0:T(8,128)(2,1)S(1)}, u32[]{:S(2)}, u32[]{:S(2)}) async-start(bf16[16,64,352]{2,1,0:T(8,128)(2,1)} %bitcast.130), calls=%async_computation.4 | async-start | bytes 1572864 | tf_op jit(solution)/shard_map/all_to_all | solution.py:987
  634.2 203.1 %reduce-scatter.9.cloned.1.call-start = ((), (), s32[]{:S(2)}) async-start(), calls=%async_computation.14 | async-start | bytes 34603008 | tf_op jit(solution)/shard_map/reduce_scatter | solution.py:1010
  676.5 25.1 %collective-permute-start.88 = (bf16[64,2048]{1,0:T(8,128)(2,1)S(1)}, bf16[64,2048]{1,0:T(8,128)(2,1)S(1)}, u32[]{:S(2)}, u32[]{:S(2)}) collective-permute-start(bf16[64,2048]{1,0:T(8,128)(2,1)S(1)} %get-tuple-element.632), channel_id=1, source_target_pairs={{0,4},{4,0},{8,12},{12,8},{1,5},{5,1},{9,13},{13,9},{2,6},{6,2},{1... | collective-permute-start | bytes 786440 | tf_op jit(solution)/shard_map/ppermute | solution.py:93
  678.4 23.2 %collective-permute-start.90 = (bf16[64,2048]{1,0:T(8,128)(2,1)S(1)}, bf16[64,2048]{1,0:T(8,128)(2,1)S(1)}, u32[]{:S(2)}, u32[]{:S(2)}) collective-permute-start(bf16[64,2048]{1,0:T(8,128)(2,1)S(1)} %get-tuple-element.633), channel_id=1, source_target_pairs={{0,12},{4,8},{8,4},{12,0},{1,13},{5,9},{9,5},{13,1},{2,14},{6,10},... | collective-permute-start | bytes 786440 | tf_op jit(solution)/shard_map/ppermute | solution.py:93
  680.8 23.3 %collective-permute-start.89 = (bf16[64,2048]{1,0:T(8,128)(2,1)S(1)}, bf16[64,2048]{1,0:T(8,128)(2,1)S(1)}, u32[]{:S(2)}, u32[]{:S(2)}) collective-permute-start(bf16[64,2048]{1,0:T(8,128)(2,1)S(1)} %get-tuple-element.634), channel_id=1, source_target_pairs={{0,8},{4,12},{8,0},{12,4},{1,9},{5,13},{9,1},{13,5},{2,10},{6,14},... | collective-permute-start | bytes 786440 | tf_op jit(solution)/shard_map/ppermute | solution.py:93
  715.7 32.3 %collective-permute-start.93 = (bf16[128,2688]{1,0:T(8,128)(2,1)}, bf16[128,2688]{1,0:T(8,128)(2,1)}, u32[]{:S(2)}, u32[]{:S(2)}) collective-permute-start(bf16[128,2688]{1,0:T(8,128)(2,1)} %get-tuple-element.614), channel_id=1, source_target_pairs={{0,2},{1,3},{2,0},{3,1},{4,6},{5,7},{6,4},{7,5},{8,10},{9,11},{10,... | collective-permute-start | bytes 2064392 | tf_op jit(solution)/shard_map/ppermute | solution.py:93
  717.2 30.8 %collective-permute-start.94 = (bf16[128,2688]{1,0:T(8,128)(2,1)}, bf16[128,2688]{1,0:T(8,128)(2,1)}, u32[]{:S(2)}, u32[]{:S(2)}) collective-permute-start(bf16[128,2688]{1,0:T(8,128)(2,1)} %get-tuple-element.615), channel_id=1, source_target_pairs={{0,3},{1,2},{2,1},{3,0},{4,7},{5,6},{6,5},{7,4},{8,11},{9,10},{10,... | collective-permute-start | bytes 2064392 | tf_op jit(solution)/shard_map/ppermute | solution.py:93
  723.0 54.2 %all-to-all-start.4 = ((bf16[4,2,256,512]{3,2,1,0:T(8,128)(2,1)}), bf16[4,2,256,512]{3,2,1,0:T(8,128)(2,1)}, u32[]{:S(2)}, u32[]{:S(2)}) async-start(bf16[4,2,256,512]{3,2,1,0:T(8,128)(2,1)} %copy_bitcast_fusion), calls=%async_computation.5 | async-start | bytes 4194304 | tf_op jit(solution)/shard_map/all_to_all | solution.py:1038
  780.1 37.7 %all-to-all-start.5 = ((bf16[8,64,512]{2,1,0:T(8,128)(2,1)}), bf16[8,64,512]{2,1,0:T(8,128)(2,1)}, u32[]{:S(2)}, u32[]{:S(2)}) async-start(bf16[8,64,512]{2,1,0:T(8,128)(2,1)} %bitcast.334), calls=%async_computation.6 | async-start | bytes 1048576 | tf_op jit(solution)/shard_map/all_to_all | solution.py:1087
  787.3 29.2 %collective-permute-start.98 = (bf16[4,64,640]{2,1,0:T(8,128)(2,1)}, bf16[4,64,640]{2,1,0:T(8,128)(2,1)}, u32[]{:S(2)}, u32[]{:S(2)}) collective-permute-start(bf16[4,64,640]{2,1,0:T(8,128)(2,1)} %get-tuple-element.628), channel_id=1, source_target_pairs={{0,3},{1,2},{2,1},{3,0},{4,7},{5,6},{6,5},{7,4},{8,11},{9,10},{10,... | collective-permute-start | bytes 983048 | tf_op jit(solution)/shard_map/ppermute | solution.py:93
  788.7 27.7 %collective-permute-start.97 = (bf16[4,64,640]{2,1,0:T(8,128)(2,1)}, bf16[4,64,640]{2,1,0:T(8,128)(2,1)}, u32[]{:S(2)}, u32[]{:S(2)}) collective-permute-start(bf16[4,64,640]{2,1,0:T(8,128)(2,1)} %get-tuple-element.629), channel_id=1, source_target_pairs={{0,2},{1,3},{2,0},{3,1},{4,6},{5,7},{6,4},{7,5},{8,10},{9,11},{10,... | collective-permute-start | bytes 983048 | tf_op jit(solution)/shard_map/ppermute | solution.py:93
  791.7 26.1 %collective-permute-start.99 = (bf16[64,2048]{1,0:T(8,128)(2,1)}, bf16[64,2048]{1,0:T(8,128)(2,1)}, u32[]{:S(2)}, u32[]{:S(2)}) collective-permute-start(bf16[64,2048]{1,0:T(8,128)(2,1)} %fusion.22), channel_id=1, source_target_pairs={{0,0},{4,1},{8,2},{12,3},{1,4},{5,5},{9,6},{13,7},{2,8},{6,9},{10,... | collective-permute-start | bytes 786440 | tf_op jit(solution)/shard_map/ppermute | solution.py:1095
  (142 other events, 1609.8 us)
Sparse Core Ops, SparseCore 0:
  9.7 18.7 all-gather.4
  30.0 25.0 all-gather.2
  593.4 10.0 reduce-scatter.4
  605.7 10.8 reduce-scatter.6
  619.3 21.4 reduce-scatter.10
  661.6 34.3 reduce-scatter.8
